TPU v7x, 256 devices: a whole 4x4x8 slice. The times are simulated.
256 devices in a mesh: gx: 8 (over z_hi, core), gy: 8 (over y, z_lo), gz: 4 (over x).
Axes of the slice: x: 4, y: 4, z: 8 (z_hi: 4, z_lo: 2; z = z_hi * 2 + z_lo), core: 2. Of those that a mesh axis runs over, the one named last changes fastest.
Arguments:
- displacement: float32 [3, 64, 128, 512], P(None, 'gx', 'gy', 'gz'), may hold values from -0.16 to 0.16
- velocity: float32 [3, 64, 128, 512], P(None, 'gx', 'gy', 'gz'), may hold values from -1.2 to 1.2
- stiffness: float32 [64, 128, 512], P('gx', 'gy', 'gz'), may hold values from 0.5 to 2
- broken: int32 [61, 64, 128, 512], P(None, 'gx', 'gy', 'gz'), may hold values 0 or 1
- borehole_id: int32 [64, 128, 512], P('gx', 'gy', 'gz'), may hold values from 0 to 7
- flags: int32 [64, 128, 512], P('gx', 'gy', 'gz'), may hold values 0 or 1
- pressure: float32 [8], replicated, may hold values from 0.5 to 4
Outputs:
- displacement_out: float32 [3, 64, 128, 512], P(None, 'gx', 'gy', 'gz')
- velocity_out: float32 [3, 64, 128, 512], P(None, 'gx', 'gy', 'gz')
- accel_out: float32 [3, 64, 128, 512], P(None, 'gx', 'gy', 'gz')
All inputs are finite; a program needn't handle non-finite values. No bound on the sum of `broken` or of `flags` on one device may be relied on, other than what follows from the above.
Results may differ from a plain program's by a relative error of at most 0.00002.
Values sent between devices are 32-bit elements; how exact they have to be, the bound alone decides.
No kernel may reach another device: no remote copies, remote signals or barrier semaphores. Data moves between devices by JAX's collectives and lax.ppermute only.
A program may use at most 192 MiB of HBM per device.

v0:
```python
import math

import jax
import jax.numpy as jnp
from jax import lax
from jax.sharding import PartitionSpec as P

STEPS = 2


C_BOND = 3.0
DT_STEP = 0.04


def shifted(block, axis, distance):
    devices = range(lax.axis_size(axis))
    route = [(i - distance, i) for i in devices if i - distance in devices]
    return lax.ppermute(block, axis, route)


def with_halo(cells, sides, width):
    for axis, dim in sides:
        count = lax.axis_size(axis)
        ends = count - 1
        head = lax.slice_in_dim(cells, 0, width, axis=dim)
        tail = lax.slice_in_dim(cells, cells.shape[dim] - width, cells.shape[dim], axis=dim)
        cells = jnp.concatenate(
            [
                lax.ppermute(tail, axis, [(i, (i + 1) % count) for i in range(ends)]),
                cells,
                lax.ppermute(head, axis, [((i + 1) % count, i) for i in range(ends)]),
            ],
            axis=dim,
        )
    return cells


def half_offsets():
    result = []
    for step_x in range(0, 4):
        for step_y in range(-3, 4):
            for step_z in range(-3, 4):
                square = step_x * step_x + step_y * step_y + step_z * step_z
                if square == 0 or square > 9:
                    continue
                if step_x > 0 or (step_x == 0 and (step_y > 0 or (step_y == 0 and step_z > 0))):
                    result.append((step_x, step_y, step_z))
    return result


def bond_force(motion_own, motion_far, stiff_own, stiff_far, weight_keep, offset):
    radial = [
        float(offset[dimension]) + (motion_far[dimension] - motion_own[dimension])
        for dimension in range(3)
    ]
    length = jnp.sqrt(radial[0] * radial[0] + radial[1] * radial[1] + radial[2] * radial[2])
    rest_length = math.sqrt(offset[0] ** 2 + offset[1] ** 2 + offset[2] ** 2)
    factor = (
        weight_keep
        * (0.5 * C_BOND)
        * (stiff_own + stiff_far)
        * ((length - rest_length) / rest_length)
        / length
    )
    return jnp.stack([factor * radial[0], factor * radial[1], factor * radial[2]])


def pore_pressure(borehole_id, flags, pressure):
    labels = jnp.arange(pressure.shape[0], dtype=jnp.int32)
    matches = borehole_id[None] == labels[:, None, None, None]
    return flags.astype(pressure.dtype) * jnp.sum(
        jnp.where(matches, pressure[:, None, None, None], 0.0), axis=0
    )


def inside_line(position, count, extent, lower_pad, upper_pad):
    lowest = position * extent - lower_pad
    places = lowest + jnp.arange(extent + lower_pad + upper_pad, dtype=jnp.int32)
    return ((places >= 0) & (places < count * extent)).astype(jnp.float32)


def inside_block(extent, lower_x):
    line_x = inside_line(lax.axis_index("gx"), lax.axis_size("gx"), extent[0], lower_x, 3)
    line_y = inside_line(lax.axis_index("gy"), lax.axis_size("gy"), extent[1], 3, 3)
    line_z = inside_line(lax.axis_index("gz"), lax.axis_size("gz"), extent[2], 3, 3)
    return line_x[:, None, None] * line_y[None, :, None] * line_z[None, None, :]


def window_of(anchor, offset, extent):
    return tuple(
        (
            slice(
                anchor[dimension] + offset[dimension],
                anchor[dimension] + offset[dimension] + extent[dimension],
            )
            for dimension in range(3)
        )
    )


def place(term, lows, full_shape):
    leading = term.ndim - 3
    widths = [(0, 0)] * leading
    for dimension in range(3):
        size_now = term.shape[leading + dimension]
        widths.append((lows[dimension], full_shape[dimension] - lows[dimension] - size_now))
    return jnp.pad(term, widths)


def pad_axis(values, axis, low, high):
    widths = [(0, 0)] * values.ndim
    widths[axis] = (low, high)
    return jnp.pad(values, widths)


def reach_upper(values):
    incoming = shifted(values[:, :3], "gx", -1)
    joined = jnp.concatenate([values, incoming], axis=1)
    return with_halo(joined, (("gy", 2), ("gz", 3)), 3)


def fold_second(values, size_y):
    interior = values[:, :, 3 : 3 + size_y]
    for direction in (1, -1):
        outgoing = values[:, :, 3 + size_y :] if direction == 1 else values[:, :, :3]
        arrived = shifted(outgoing, "gy", direction)
        if direction == 1:
            interior = interior + pad_axis(arrived, 2, 0, size_y - 3)
        else:
            interior = interior + pad_axis(arrived, 2, size_y - 3, 0)
    return interior


def fold_third(values, size_z):
    interior = values[:, :, :, 3 : 3 + size_z]
    for direction in (1, -1):
        outgoing = values[:, :, :, 3 + size_z :] if direction == 1 else values[:, :, :, :3]
        arrived = shifted(outgoing, "gz", direction)
        if direction == 1:
            interior = interior + pad_axis(arrived, 3, 0, size_z - 3)
        else:
            interior = interior + pad_axis(arrived, 3, size_z - 3, 0)
    return interior


def on_device(displacement, velocity, stiffness, broken, borehole_id, flags, pressure):
    extent = stiffness.shape
    offsets = half_offsets()
    pore_field = pore_pressure(borehole_id, flags, pressure)
    static = jnp.stack([stiffness, pore_field])
    anchor = (0, 3, 3)
    inside = inside_block(extent, 0)
    full_shape = inside.shape
    static_ext = reach_upper(static)
    stiff_ext = static_ext[0]
    pore_ext = static_ext[1]
    own_parts = []
    ext_parts = []
    for dimension in range(3):
        offset = tuple((1 if other == dimension else 0 for other in range(3)))
        window = window_of(anchor, offset, extent)
        half_diff = -0.5 * (pore_ext[window] - pore_field) * inside[window]
        own_parts.append(half_diff)
        lows = tuple((anchor[other] + offset[other] for other in range(3)))
        ext_parts.append(place(half_diff, lows, full_shape))
    press_own = jnp.stack(own_parts)
    press_ext = jnp.stack(ext_parts)

    def evaluate(motion):
        motion_ext = reach_upper(motion)
        summed = press_own
        reaction = press_ext
        for bond_index, offset in enumerate(offsets):
            window = window_of(anchor, offset, extent)
            lows = tuple((anchor[other] + offset[other] for other in range(3)))
            weight_keep = (1 - broken[bond_index]).astype(jnp.float32) * inside[window]
            bond_term = bond_force(
                motion,
                motion_ext[(slice(None),) + window],
                stiffness,
                stiff_ext[window],
                weight_keep,
                offset,
            )
            summed = summed + bond_term
            reaction = reaction - place(bond_term, lows, full_shape)
        reaction = reaction + place(summed, anchor, full_shape)
        outgoing = reaction[:, extent[0] :]
        arrived = shifted(outgoing, "gx", 1)
        interior = reaction[:, : extent[0]] + pad_axis(arrived, 1, 0, extent[0] - 3)
        return fold_third(fold_second(interior, extent[1]), extent[2])

    accel = evaluate(displacement)
    motion = displacement
    speed = velocity
    for step_index in range(STEPS):
        halfway = speed + 0.5 * DT_STEP * accel
        motion = motion + DT_STEP * halfway
        accel = evaluate(motion)
        speed = halfway + 0.5 * DT_STEP * accel
    return (motion, speed, accel)


def solution(mesh):
    in_specs = (
        P(None, "gx", "gy", "gz"),
        P(None, "gx", "gy", "gz"),
        P("gx", "gy", "gz"),
        P(None, "gx", "gy", "gz"),
        P("gx", "gy", "gz"),
        P("gx", "gy", "gz"),
        P(),
    )
    out_specs = (P(None, "gx", "gy", "gz"), P(None, "gx", "gy", "gz"), P(None, "gx", "gy", "gz"))
    return jax.shard_map(
        on_device, mesh=mesh, in_specs=in_specs, out_specs=out_specs, check_vma=False
    )
```

profile of v0, /device:TPU:92, one launch (start us, length us, event | category | flops | bytes accessed | tf_op | source)
XLA Modules:
  0.0 273.9 jit_solution(9823617318919769454)
XLA Ops:
  10.2 4.0 %collective-permute-start.2 = (f32[2,11,3,128]{3,2,1,0:T(4,128)S(1)}, f32[2,11,3,128]{3,2,1,0:T(4,128)S(1)}, u32[]{:S(2)}, u32[]{:S(2)}) collective-permute-start(f32[2,11,3,128]{3,2,1,0:T(4,128)S(1)} %get-tuple-element.1310), channel_id=1, source_target_pairs={{4,0},{8,4},{12,8},{16,12},{20,16},{24,20},{28,24},{5,1},{9,5},{13... | collective-permute-start | bytes 101384 | tf_op jit(solution)/shard_map/ppermute | solution.py:31
  16.1 5.3 %collective-permute-done.1 = f32[2,11,3,128]{3,2,1,0:T(4,128)S(1)} collective-permute-done((f32[2,11,3,128]{3,2,1,0:T(4,128)S(1)}, f32[2,11,3,128]{3,2,1,0:T(4,128)S(1)}, u32[]{:S(2)}, u32[]{:S(2)}) %collective-permute-start.1) | collective-permute-done | bytes 33824 | tf_op jit(solution)/shard_map/ppermute | solution.py:29
  24.9 3.4 %collective-permute-start.3 = (f32[2,11,22,3]{3,2,1,0:T(8,128)S(1)}, f32[2,11,22,3]{3,2,1,0:T(8,128)S(1)}, u32[]{:S(2)}, u32[]{:S(2)}) collective-permute-start(f32[2,11,22,3]{3,2,1,0:T(8,128)S(1)} %get-tuple-element.1297), channel_id=1, source_target_pairs={{0,1},{1,2},{2,3},{4,5},{5,6},{6,7},{8,9},{9,10},{10,11},{12,13},{... | collective-permute-start | bytes 17432 | tf_op jit(solution)/shard_map/ppermute | solution.py:29
  30.3 3.9 %collective-permute-start.6 = (f32[3,11,3,128]{3,2,1,0:T(4,128)S(1)}, f32[3,11,3,128]{3,2,1,0:T(4,128)S(1)}, u32[]{:S(2)}, u32[]{:S(2)}) collective-permute-start(f32[3,11,3,128]{3,2,1,0:T(4,128)S(1)} %get-tuple-element.1295), channel_id=1, source_target_pairs={{0,4},{4,8},{8,12},{12,16},{16,20},{20,24},{24,28},{1,5},{5,9},{9,... | collective-permute-start | bytes 152072 | tf_op jit(solution)/shard_map/ppermute | solution.py:29
  45.3 4.0 %collective-permute-done.9 = f32[3,11,22,3]{3,2,1,0:T(8,128)S(1)} collective-permute-done((f32[3,11,22,3]{3,2,1,0:T(8,128)S(1)}, f32[3,11,22,3]{3,2,1,0:T(8,128)S(1)}, u32[]{:S(2)}, u32[]{:S(2)}) %collective-permute-start.9) | collective-permute-done | bytes 8744 | tf_op jit(solution)/shard_map/ppermute | solution.py:29
  49.3 3.1 %collective-permute-done.8 = f32[3,11,22,3]{3,2,1,0:T(8,128)S(1)} collective-permute-done((f32[3,11,22,3]{3,2,1,0:T(8,128)S(1)}, f32[3,11,22,3]{3,2,1,0:T(8,128)S(1)}, u32[]{:S(2)}, u32[]{:S(2)}) %collective-permute-start.8) | collective-permute-done | bytes 8744 | tf_op jit(solution)/shard_map/ppermute | solution.py:31
  65.0 10.7 %pad_add_fusion.2 = f32[3,11,22,134]{3,2,1,0:T(8,128)S(1)} fusion(f32[3,8,16,128]{3,2,1,0:T(8,128)S(1)} %add_add_fusion.3, f32[3,8,16,128]{3,2,1,0:T(8,128)S(1)} %get-tuple-element.1316, f32[3,8,16,128]{3,2,1,0:T(8,128)S(1)} %get-tuple-element.1320, f32[3,8,16,128]{3,2,1,0:T(8,128)S(1)} %get-tuple-element.1324, ...), kind=kLoop, calls=%fused_computation.91 | loop fusion | flops 6226176 | bytes 12967968 | tf_op jit(solution)/shard_map/add | solution.py:187
  77.8 7.1 %collective-permute-done.10 = f32[3,3,22,134]{3,2,1,0:T(8,128)S(1)} collective-permute-done((f32[3,3,22,134]{3,2,1,0:T(8,128)S(1)}, f32[3,3,22,134]{3,2,1,0:T(8,128)S(1)}, u32[]{:S(2)}, u32[]{:S(2)}) %collective-permute-start.10) | collective-permute-done | bytes 106160 | tf_op jit(solution)/shard_map/ppermute | solution.py:18
  85.0 3.3 %collective-permute-start.12 = (f32[3,8,3,134]{3,2,1,0:T(4,128)S(1)}, f32[3,8,3,134]{3,2,1,0:T(4,128)S(1)}, u32[]{:S(2)}, u32[]{:S(2)}) collective-permute-start(f32[3,8,3,134]{3,2,1,0:T(4,128)S(1)} %get-tuple-element.1211), channel_id=1, source_target_pairs={{4,0},{8,4},{12,8},{16,12},{20,16},{24,20},{28,24},{5,1},{9,5},{13... | collective-permute-start | bytes 115784 | tf_op jit(solution)/shard_map/ppermute | solution.py:18
  91.5 4.2 %collective-permute-done.11 = f32[3,8,3,134]{3,2,1,0:T(4,128)S(1)} collective-permute-done((f32[3,8,3,134]{3,2,1,0:T(4,128)S(1)}, f32[3,8,3,134]{3,2,1,0:T(4,128)S(1)}, u32[]{:S(2)}, u32[]{:S(2)}) %collective-permute-start.11) | collective-permute-done | bytes 38624 | tf_op jit(solution)/shard_map/ppermute | solution.py:18
  96.0 3.1 %collective-permute-start.14 = (f32[3,8,16,3]{3,2,1,0:T(8,128)S(1)}, f32[3,8,16,3]{3,2,1,0:T(8,128)S(1)}, u32[]{:S(2)}, u32[]{:S(2)}) collective-permute-start(f32[3,8,16,3]{3,2,1,0:T(8,128)S(1)} %get-tuple-element.1266), channel_id=1, source_target_pairs={{1,0},{2,1},{3,2},{5,4},{6,5},{7,6},{9,8},{10,9},{11,10},{13,12},{... | collective-permute-start | bytes 13832 | tf_op jit(solution)/shard_map/ppermute | solution.py:18
  103.5 3.1 %collective-permute-done.13 = f32[3,8,16,3]{3,2,1,0:T(8,128)S(1)} collective-permute-done((f32[3,8,16,3]{3,2,1,0:T(8,128)S(1)}, f32[3,8,16,3]{3,2,1,0:T(8,128)S(1)}, u32[]{:S(2)}, u32[]{:S(2)}) %collective-permute-start.13) | collective-permute-done | bytes 4640 | tf_op jit(solution)/shard_map/ppermute | solution.py:18
  112.7 3.9 %collective-permute-start.16 = (f32[3,11,3,128]{3,2,1,0:T(4,128)S(1)}, f32[3,11,3,128]{3,2,1,0:T(4,128)S(1)}, u32[]{:S(2)}, u32[]{:S(2)}) collective-permute-start(f32[3,11,3,128]{3,2,1,0:T(4,128)S(1)} %get-tuple-element.1293), channel_id=1, source_target_pairs={{0,4},{4,8},{8,12},{12,16},{16,20},{20,24},{24,28},{1,5},{5,9},{9,... | collective-permute-start | bytes 152072 | tf_op jit(solution)/shard_map/ppermute | solution.py:29
  117.0 3.5 %collective-permute-done.16 = f32[3,11,3,128]{3,2,1,0:T(4,128)S(1)} collective-permute-done((f32[3,11,3,128]{3,2,1,0:T(4,128)S(1)}, f32[3,11,3,128]{3,2,1,0:T(4,128)S(1)}, u32[]{:S(2)}, u32[]{:S(2)}) %collective-permute-start.16) | collective-permute-done | bytes 50720 | tf_op jit(solution)/shard_map/ppermute | solution.py:29
  123.3 3.5 %collective-permute-start.18 = (f32[3,11,22,3]{3,2,1,0:T(8,128)S(1)}, f32[3,11,22,3]{3,2,1,0:T(8,128)S(1)}, u32[]{:S(2)}, u32[]{:S(2)}) collective-permute-start(f32[3,11,22,3]{3,2,1,0:T(8,128)S(1)} %get-tuple-element.1256), channel_id=1, source_target_pairs={{1,0},{2,1},{3,2},{5,4},{6,5},{7,6},{9,8},{10,9},{11,10},{13,12},{... | collective-permute-start | bytes 26144 | tf_op jit(solution)/shard_map/ppermute | solution.py:31
  127.9 5.9 %collective-permute-done.19 = f32[3,11,22,3]{3,2,1,0:T(8,128)S(1)} collective-permute-done((f32[3,11,22,3]{3,2,1,0:T(8,128)S(1)}, f32[3,11,22,3]{3,2,1,0:T(8,128)S(1)}, u32[]{:S(2)}, u32[]{:S(2)}) %collective-permute-start.19) | collective-permute-done | bytes 8744 | tf_op jit(solution)/shard_map/ppermute | solution.py:29
  147.8 10.7 %pad_add_fusion.1 = f32[3,11,22,134]{3,2,1,0:T(8,128)S(1)} fusion(f32[3,8,16,128]{3,2,1,0:T(8,128)S(1)} %add_add_fusion.2, f32[3,8,16,128]{3,2,1,0:T(8,128)S(1)} %pad_maximum_fusion.133, f32[3,8,16,128]{3,2,1,0:T(8,128)S(1)} %pad_maximum_fusion.132, f32[3,8,16,128]{3,2,1,0:T(8,128)S(1)} %pad_maximum_fusion.131, ...), kind=kLoop, calls=%fused_computation.90 | loop fusion | flops 6226176 | bytes 12967968 | tf_op jit(solution)/shard_map/add | solution.py:187
  161.0 6.8 %collective-permute-done.20 = f32[3,3,22,134]{3,2,1,0:T(8,128)S(1)} collective-permute-done((f32[3,3,22,134]{3,2,1,0:T(8,128)S(1)}, f32[3,3,22,134]{3,2,1,0:T(8,128)S(1)}, u32[]{:S(2)}, u32[]{:S(2)}) %collective-permute-start.20) | collective-permute-done | bytes 106160 | tf_op jit(solution)/shard_map/ppermute | solution.py:18
  167.9 3.5 %collective-permute-start.22 = (f32[3,8,3,134]{3,2,1,0:T(4,128)S(1)}, f32[3,8,3,134]{3,2,1,0:T(4,128)S(1)}, u32[]{:S(2)}, u32[]{:S(2)}) collective-permute-start(f32[3,8,3,134]{3,2,1,0:T(4,128)S(1)} %get-tuple-element.1209), channel_id=1, source_target_pairs={{4,0},{8,4},{12,8},{16,12},{20,16},{24,20},{28,24},{5,1},{9,5},{13... | collective-permute-start | bytes 115784 | tf_op jit(solution)/shard_map/ppermute | solution.py:18
  174.4 4.4 %collective-permute-done.21 = f32[3,8,3,134]{3,2,1,0:T(4,128)S(1)} collective-permute-done((f32[3,8,3,134]{3,2,1,0:T(4,128)S(1)}, f32[3,8,3,134]{3,2,1,0:T(4,128)S(1)}, u32[]{:S(2)}, u32[]{:S(2)}) %collective-permute-start.21) | collective-permute-done | bytes 38624 | tf_op jit(solution)/shard_map/ppermute | solution.py:18
  179.0 3.7 %collective-permute-start.24 = (f32[3,8,16,3]{3,2,1,0:T(8,128)S(1)}, f32[3,8,16,3]{3,2,1,0:T(8,128)S(1)}, u32[]{:S(2)}, u32[]{:S(2)}) collective-permute-start(f32[3,8,16,3]{3,2,1,0:T(8,128)S(1)} %get-tuple-element.1264), channel_id=1, source_target_pairs={{1,0},{2,1},{3,2},{5,4},{6,5},{7,6},{9,8},{10,9},{11,10},{13,12},{... | collective-permute-start | bytes 13832 | tf_op jit(solution)/shard_map/ppermute | solution.py:18
  187.0 4.1 %collective-permute-done.23 = f32[3,8,16,3]{3,2,1,0:T(8,128)S(1)} collective-permute-done((f32[3,8,16,3]{3,2,1,0:T(8,128)S(1)}, f32[3,8,16,3]{3,2,1,0:T(8,128)S(1)}, u32[]{:S(2)}, u32[]{:S(2)}) %collective-permute-start.23) | collective-permute-done | bytes 4640 | tf_op jit(solution)/shard_map/ppermute | solution.py:18
  197.1 3.9 %collective-permute-start.26 = (f32[3,11,3,128]{3,2,1,0:T(4,128)S(1)}, f32[3,11,3,128]{3,2,1,0:T(4,128)S(1)}, u32[]{:S(2)}, u32[]{:S(2)}) collective-permute-start(f32[3,11,3,128]{3,2,1,0:T(4,128)S(1)} %get-tuple-element.1283), channel_id=1, source_target_pairs={{0,4},{4,8},{8,12},{12,16},{16,20},{20,24},{24,28},{1,5},{5,9},{9,... | collective-permute-start | bytes 152072 | tf_op jit(solution)/shard_map/ppermute | solution.py:29
  201.4 3.1 %collective-permute-done.26 = f32[3,11,3,128]{3,2,1,0:T(4,128)S(1)} collective-permute-done((f32[3,11,3,128]{3,2,1,0:T(4,128)S(1)}, f32[3,11,3,128]{3,2,1,0:T(4,128)S(1)}, u32[]{:S(2)}, u32[]{:S(2)}) %collective-permute-start.26) | collective-permute-done | bytes 50720 | tf_op jit(solution)/shard_map/ppermute | solution.py:29
  207.4 3.4 %collective-permute-start.28 = (f32[3,11,22,3]{3,2,1,0:T(8,128)S(1)}, f32[3,11,22,3]{3,2,1,0:T(8,128)S(1)}, u32[]{:S(2)}, u32[]{:S(2)}) collective-permute-start(f32[3,11,22,3]{3,2,1,0:T(8,128)S(1)} %get-tuple-element.1252), channel_id=1, source_target_pairs={{1,0},{2,1},{3,2},{5,4},{6,5},{7,6},{9,8},{10,9},{11,10},{13,12},{... | collective-permute-start | bytes 26144 | tf_op jit(solution)/shard_map/ppermute | solution.py:31
  211.8 5.4 %collective-permute-done.29 = f32[3,11,22,3]{3,2,1,0:T(8,128)S(1)} collective-permute-done((f32[3,11,22,3]{3,2,1,0:T(8,128)S(1)}, f32[3,11,22,3]{3,2,1,0:T(8,128)S(1)}, u32[]{:S(2)}, u32[]{:S(2)}) %collective-permute-start.29) | collective-permute-done | bytes 8744 | tf_op jit(solution)/shard_map/ppermute | solution.py:29
  217.3 3.4 %collective-permute-done.28 = f32[3,11,22,3]{3,2,1,0:T(8,128)S(1)} collective-permute-done((f32[3,11,22,3]{3,2,1,0:T(8,128)S(1)}, f32[3,11,22,3]{3,2,1,0:T(8,128)S(1)}, u32[]{:S(2)}, u32[]{:S(2)}) %collective-permute-start.28) | collective-permute-done | bytes 8744 | tf_op jit(solution)/shard_map/ppermute | solution.py:31
  231.5 10.7 %pad_add_fusion = f32[3,11,22,134]{3,2,1,0:T(8,128)S(1)} fusion(f32[3,8,16,128]{3,2,1,0:T(8,128)S(1)} %add_add_fusion.1, f32[3,8,16,128]{3,2,1,0:T(8,128)S(1)} %pad_maximum_fusion.194, f32[3,8,16,128]{3,2,1,0:T(8,128)S(1)} %pad_maximum_fusion.193, f32[3,8,16,128]{3,2,1,0:T(8,128)S(1)} %pad_maximum_fusion.192, f32[3,8,16,128]{3,2,1,0:T(8,128)S(1)} %pad_maximum_fusion.191, ...), kind=kLoop, calls=%fused_computation.89 | loop fusion | flops 6226176 | bytes 12967968 | tf_op jit(solution)/shard_map/add | solution.py:187
  244.8 6.6 %collective-permute-done.30 = f32[3,3,22,134]{3,2,1,0:T(8,128)S(1)} collective-permute-done((f32[3,3,22,134]{3,2,1,0:T(8,128)S(1)}, f32[3,3,22,134]{3,2,1,0:T(8,128)S(1)}, u32[]{:S(2)}, u32[]{:S(2)}) %collective-permute-start.30) | collective-permute-done | bytes 106160 | tf_op jit(solution)/shard_map/ppermute | solution.py:18
  258.0 3.7 %collective-permute-done.31 = f32[3,8,3,134]{3,2,1,0:T(4,128)S(1)} collective-permute-done((f32[3,8,3,134]{3,2,1,0:T(4,128)S(1)}, f32[3,8,3,134]{3,2,1,0:T(4,128)S(1)}, u32[]{:S(2)}, u32[]{:S(2)}) %collective-permute-start.31) | collective-permute-done | bytes 38624 | tf_op jit(solution)/shard_map/ppermute | solution.py:18
  261.9 3.3 %collective-permute-start.34 = (f32[3,8,16,3]{3,2,1,0:T(8,128)S(1)}, f32[3,8,16,3]{3,2,1,0:T(8,128)S(1)}, u32[]{:S(2)}, u32[]{:S(2)}) collective-permute-start(f32[3,8,16,3]{3,2,1,0:T(8,128)S(1)} %get-tuple-element.1262), channel_id=1, source_target_pairs={{1,0},{2,1},{3,2},{5,4},{6,5},{7,6},{9,8},{10,9},{11,10},{13,12},{... | collective-permute-start | bytes 13832 | tf_op jit(solution)/shard_map/ppermute | solution.py:18
  269.5 3.3 %collective-permute-done.33 = f32[3,8,16,3]{3,2,1,0:T(8,128)S(1)} collective-permute-done((f32[3,8,16,3]{3,2,1,0:T(8,128)S(1)}, f32[3,8,16,3]{3,2,1,0:T(8,128)S(1)}, u32[]{:S(2)}, u32[]{:S(2)}) %collective-permute-start.33) | collective-permute-done | bytes 4640 | tf_op jit(solution)/shard_map/ppermute | solution.py:18
  (407 shorter events, 118.3 us)
Async XLA Ops:
  3.3 6.1 %collective-permute-start = (f32[2,3,16,128]{3,2,1,0:T(8,128)S(1)}, f32[2,3,16,128]{3,2,1,0:T(8,128)S(1)}, u32[]{:S(2)}, u32[]{:S(2)}) collective-permute-start(f32[2,3,16,128]{3,2,1,0:T(8,128)S(1)} %pad_maximum_fusion.199), channel_id=1, source_target_pairs={{32,0},{64,32},{96,64},{128,96},{160,128},{192,160},{224,192},{33,... | collective-permute-start | bytes 147464 | tf_op jit(solution)/shard_map/ppermute | solution.py:18
  6.1 10.0 %collective-permute-start.5 = (f32[3,3,16,128]{3,2,1,0:T(8,128)S(1)}, f32[3,3,16,128]{3,2,1,0:T(8,128)S(1)}, u32[]{:S(2)}, u32[]{:S(2)}) collective-permute-start(f32[3,3,16,128]{3,2,1,0:T(8,128)S(1)} %slice.4200), channel_id=1, source_target_pairs={{32,0},{64,32},{96,64},{128,96},{160,128},{192,160},{224,192},{33,... | collective-permute-start | bytes 221192 | tf_op jit(solution)/shard_map/ppermute | solution.py:18
  14.2 7.2 %collective-permute-start.1 = (f32[2,11,3,128]{3,2,1,0:T(4,128)S(1)}, f32[2,11,3,128]{3,2,1,0:T(4,128)S(1)}, u32[]{:S(2)}, u32[]{:S(2)}) collective-permute-start(f32[2,11,3,128]{3,2,1,0:T(4,128)S(1)} %get-tuple-element.1309), channel_id=1, source_target_pairs={{0,4},{4,8},{8,12},{12,16},{16,20},{20,24},{24,28},{1,5},{5,9},{9,... | collective-permute-start | bytes 101384 | tf_op jit(solution)/shard_map/ppermute | solution.py:29
  22.4 11.8 %collective-permute-start.4 = (f32[2,11,22,3]{3,2,1,0:T(8,128)S(1)}, f32[2,11,22,3]{3,2,1,0:T(8,128)S(1)}, u32[]{:S(2)}, u32[]{:S(2)}) collective-permute-start(f32[2,11,22,3]{3,2,1,0:T(8,128)S(1)} %get-tuple-element.1298), channel_id=1, source_target_pairs={{1,0},{2,1},{3,2},{5,4},{6,5},{7,6},{9,8},{10,9},{11,10},{13,12},{... | collective-permute-start | bytes 17432 | tf_op jit(solution)/shard_map/ppermute | solution.py:31
  24.9 10.1 %collective-permute-start.3 = (f32[2,11,22,3]{3,2,1,0:T(8,128)S(1)}, f32[2,11,22,3]{3,2,1,0:T(8,128)S(1)}, u32[]{:S(2)}, u32[]{:S(2)}) collective-permute-start(f32[2,11,22,3]{3,2,1,0:T(8,128)S(1)} %get-tuple-element.1297), channel_id=1, source_target_pairs={{0,1},{1,2},{2,3},{4,5},{5,6},{6,7},{8,9},{9,10},{10,11},{12,13},{... | collective-permute-start | bytes 17432 | tf_op jit(solution)/shard_map/ppermute | solution.py:29
  28.3 8.6 %collective-permute-start.7 = (f32[3,11,3,128]{3,2,1,0:T(4,128)S(1)}, f32[3,11,3,128]{3,2,1,0:T(4,128)S(1)}, u32[]{:S(2)}, u32[]{:S(2)}) collective-permute-start(f32[3,11,3,128]{3,2,1,0:T(4,128)S(1)} %get-tuple-element.1296), channel_id=1, source_target_pairs={{4,0},{8,4},{12,8},{16,12},{20,16},{24,20},{28,24},{5,1},{9,5},{13... | collective-permute-start | bytes 152072 | tf_op jit(solution)/shard_map/ppermute | solution.py:31
  30.3 7.1 %collective-permute-start.6 = (f32[3,11,3,128]{3,2,1,0:T(4,128)S(1)}, f32[3,11,3,128]{3,2,1,0:T(4,128)S(1)}, u32[]{:S(2)}, u32[]{:S(2)}) collective-permute-start(f32[3,11,3,128]{3,2,1,0:T(4,128)S(1)} %get-tuple-element.1295), channel_id=1, source_target_pairs={{0,4},{4,8},{8,12},{12,16},{16,20},{20,24},{24,28},{1,5},{5,9},{9,... | collective-permute-start | bytes 152072 | tf_op jit(solution)/shard_map/ppermute | solution.py:29
  37.6 11.8 %collective-permute-start.9 = (f32[3,11,22,3]{3,2,1,0:T(8,128)S(1)}, f32[3,11,22,3]{3,2,1,0:T(8,128)S(1)}, u32[]{:S(2)}, u32[]{:S(2)}) collective-permute-start(f32[3,11,22,3]{3,2,1,0:T(8,128)S(1)} %get-tuple-element.1259), channel_id=1, source_target_pairs={{0,1},{1,2},{2,3},{4,5},{5,6},{6,7},{8,9},{9,10},{10,11},{12,13},{... | collective-permute-start | bytes 26144 | tf_op jit(solution)/shard_map/ppermute | solution.py:29
  40.6 11.9 %collective-permute-start.8 = (f32[3,11,22,3]{3,2,1,0:T(8,128)S(1)}, f32[3,11,22,3]{3,2,1,0:T(8,128)S(1)}, u32[]{:S(2)}, u32[]{:S(2)}) collective-permute-start(f32[3,11,22,3]{3,2,1,0:T(8,128)S(1)} %get-tuple-element.1260), channel_id=1, source_target_pairs={{1,0},{2,1},{3,2},{5,4},{6,5},{7,6},{9,8},{10,9},{11,10},{13,12},{... | collective-permute-start | bytes 26144 | tf_op jit(solution)/shard_map/ppermute | solution.py:31
  75.7 9.2 %collective-permute-start.10 = (f32[3,3,22,134]{3,2,1,0:T(8,128)S(1)}, f32[3,3,22,134]{3,2,1,0:T(8,128)S(1)}, u32[]{:S(2)}, u32[]{:S(2)}) collective-permute-start(f32[3,3,22,134]{3,2,1,0:T(8,128)S(1)} %slice.5321), channel_id=1, source_target_pairs={{0,32},{32,64},{64,96},{96,128},{128,160},{160,192},{192,224},{1,3... | collective-permute-start | bytes 318392 | tf_op jit(solution)/shard_map/ppermute | solution.py:18
  85.0 6.5 %collective-permute-start.12 = (f32[3,8,3,134]{3,2,1,0:T(4,128)S(1)}, f32[3,8,3,134]{3,2,1,0:T(4,128)S(1)}, u32[]{:S(2)}, u32[]{:S(2)}) collective-permute-start(f32[3,8,3,134]{3,2,1,0:T(4,128)S(1)} %get-tuple-element.1211), channel_id=1, source_target_pairs={{4,0},{8,4},{12,8},{16,12},{20,16},{24,20},{28,24},{5,1},{9,5},{13... | collective-permute-start | bytes 115784 | tf_op jit(solution)/shard_map/ppermute | solution.py:18
  88.3 7.4 %collective-permute-start.11 = (f32[3,8,3,134]{3,2,1,0:T(4,128)S(1)}, f32[3,8,3,134]{3,2,1,0:T(4,128)S(1)}, u32[]{:S(2)}, u32[]{:S(2)}) collective-permute-start(f32[3,8,3,134]{3,2,1,0:T(4,128)S(1)} %get-tuple-element.1210), channel_id=1, source_target_pairs={{0,4},{4,8},{8,12},{12,16},{16,20},{20,24},{24,28},{1,5},{5,9},{9,... | collective-permute-start | bytes 115784 | tf_op jit(solution)/shard_map/ppermute | solution.py:18
  96.0 7.6 %collective-permute-start.14 = (f32[3,8,16,3]{3,2,1,0:T(8,128)S(1)}, f32[3,8,16,3]{3,2,1,0:T(8,128)S(1)}, u32[]{:S(2)}, u32[]{:S(2)}) collective-permute-start(f32[3,8,16,3]{3,2,1,0:T(8,128)S(1)} %get-tuple-element.1266), channel_id=1, source_target_pairs={{1,0},{2,1},{3,2},{5,4},{6,5},{7,6},{9,8},{10,9},{11,10},{13,12},{... | collective-permute-start | bytes 13832 | tf_op jit(solution)/shard_map/ppermute | solution.py:18
  99.1 7.6 %collective-permute-start.13 = (f32[3,8,16,3]{3,2,1,0:T(8,128)S(1)}, f32[3,8,16,3]{3,2,1,0:T(8,128)S(1)}, u32[]{:S(2)}, u32[]{:S(2)}) collective-permute-start(f32[3,8,16,3]{3,2,1,0:T(8,128)S(1)} %get-tuple-element.1265), channel_id=1, source_target_pairs={{0,1},{1,2},{2,3},{4,5},{5,6},{6,7},{8,9},{9,10},{10,11},{12,13},{... | collective-permute-start | bytes 13832 | tf_op jit(solution)/shard_map/ppermute | solution.py:18
  110.8 6.2 %collective-permute-start.17 = (f32[3,11,3,128]{3,2,1,0:T(4,128)S(1)}, f32[3,11,3,128]{3,2,1,0:T(4,128)S(1)}, u32[]{:S(2)}, u32[]{:S(2)}) collective-permute-start(f32[3,11,3,128]{3,2,1,0:T(4,128)S(1)} %get-tuple-element.1294), channel_id=1, source_target_pairs={{4,0},{8,4},{12,8},{16,12},{20,16},{24,20},{28,24},{5,1},{9,5},{13... | collective-permute-start | bytes 152072 | tf_op jit(solution)/shard_map/ppermute | solution.py:31
  112.7 7.8 %collective-permute-start.16 = (f32[3,11,3,128]{3,2,1,0:T(4,128)S(1)}, f32[3,11,3,128]{3,2,1,0:T(4,128)S(1)}, u32[]{:S(2)}, u32[]{:S(2)}) collective-permute-start(f32[3,11,3,128]{3,2,1,0:T(4,128)S(1)} %get-tuple-element.1293), channel_id=1, source_target_pairs={{0,4},{4,8},{8,12},{12,16},{16,20},{20,24},{24,28},{1,5},{5,9},{9,... | collective-permute-start | bytes 152072 | tf_op jit(solution)/shard_map/ppermute | solution.py:29
  120.8 13.1 %collective-permute-start.19 = (f32[3,11,22,3]{3,2,1,0:T(8,128)S(1)}, f32[3,11,22,3]{3,2,1,0:T(8,128)S(1)}, u32[]{:S(2)}, u32[]{:S(2)}) collective-permute-start(f32[3,11,22,3]{3,2,1,0:T(8,128)S(1)} %get-tuple-element.1255), channel_id=1, source_target_pairs={{0,1},{1,2},{2,3},{4,5},{5,6},{6,7},{8,9},{9,10},{10,11},{12,13},{... | collective-permute-start | bytes 26144 | tf_op jit(solution)/shard_map/ppermute | solution.py:29
  123.3 13.4 %collective-permute-start.18 = (f32[3,11,22,3]{3,2,1,0:T(8,128)S(1)}, f32[3,11,22,3]{3,2,1,0:T(8,128)S(1)}, u32[]{:S(2)}, u32[]{:S(2)}) collective-permute-start(f32[3,11,22,3]{3,2,1,0:T(8,128)S(1)} %get-tuple-element.1256), channel_id=1, source_target_pairs={{1,0},{2,1},{3,2},{5,4},{6,5},{7,6},{9,8},{10,9},{11,10},{13,12},{... | collective-permute-start | bytes 26144 | tf_op jit(solution)/shard_map/ppermute | solution.py:31
  158.5 9.3 %collective-permute-start.20 = (f32[3,3,22,134]{3,2,1,0:T(8,128)S(1)}, f32[3,3,22,134]{3,2,1,0:T(8,128)S(1)}, u32[]{:S(2)}, u32[]{:S(2)}) collective-permute-start(f32[3,3,22,134]{3,2,1,0:T(8,128)S(1)} %slice.5529), channel_id=1, source_target_pairs={{0,32},{32,64},{64,96},{96,128},{128,160},{160,192},{192,224},{1,3... | collective-permute-start | bytes 318392 | tf_op jit(solution)/shard_map/ppermute | solution.py:18
  167.9 6.5 %collective-permute-start.22 = (f32[3,8,3,134]{3,2,1,0:T(4,128)S(1)}, f32[3,8,3,134]{3,2,1,0:T(4,128)S(1)}, u32[]{:S(2)}, u32[]{:S(2)}) collective-permute-start(f32[3,8,3,134]{3,2,1,0:T(4,128)S(1)} %get-tuple-element.1209), channel_id=1, source_target_pairs={{4,0},{8,4},{12,8},{16,12},{20,16},{24,20},{28,24},{5,1},{9,5},{13... | collective-permute-start | bytes 115784 | tf_op jit(solution)/shard_map/ppermute | solution.py:18
  171.4 7.4 %collective-permute-start.21 = (f32[3,8,3,134]{3,2,1,0:T(4,128)S(1)}, f32[3,8,3,134]{3,2,1,0:T(4,128)S(1)}, u32[]{:S(2)}, u32[]{:S(2)}) collective-permute-start(f32[3,8,3,134]{3,2,1,0:T(4,128)S(1)} %get-tuple-element.1208), channel_id=1, source_target_pairs={{0,4},{4,8},{8,12},{12,16},{16,20},{20,24},{24,28},{1,5},{5,9},{9,... | collective-permute-start | bytes 115784 | tf_op jit(solution)/shard_map/ppermute | solution.py:18
  179.0 7.9 %collective-permute-start.24 = (f32[3,8,16,3]{3,2,1,0:T(8,128)S(1)}, f32[3,8,16,3]{3,2,1,0:T(8,128)S(1)}, u32[]{:S(2)}, u32[]{:S(2)}) collective-permute-start(f32[3,8,16,3]{3,2,1,0:T(8,128)S(1)} %get-tuple-element.1264), channel_id=1, source_target_pairs={{1,0},{2,1},{3,2},{5,4},{6,5},{7,6},{9,8},{10,9},{11,10},{13,12},{... | collective-permute-start | bytes 13832 | tf_op jit(solution)/shard_map/ppermute | solution.py:18
  182.7 8.4 %collective-permute-start.23 = (f32[3,8,16,3]{3,2,1,0:T(8,128)S(1)}, f32[3,8,16,3]{3,2,1,0:T(8,128)S(1)}, u32[]{:S(2)}, u32[]{:S(2)}) collective-permute-start(f32[3,8,16,3]{3,2,1,0:T(8,128)S(1)} %get-tuple-element.1263), channel_id=1, source_target_pairs={{0,1},{1,2},{2,3},{4,5},{5,6},{6,7},{8,9},{9,10},{10,11},{12,13},{... | collective-permute-start | bytes 13832 | tf_op jit(solution)/shard_map/ppermute | solution.py:18
  195.2 6.2 %collective-permute-start.27 = (f32[3,11,3,128]{3,2,1,0:T(4,128)S(1)}, f32[3,11,3,128]{3,2,1,0:T(4,128)S(1)}, u32[]{:S(2)}, u32[]{:S(2)}) collective-permute-start(f32[3,11,3,128]{3,2,1,0:T(4,128)S(1)} %get-tuple-element.1284), channel_id=1, source_target_pairs={{4,0},{8,4},{12,8},{16,12},{20,16},{24,20},{28,24},{5,1},{9,5},{13... | collective-permute-start | bytes 152072 | tf_op jit(solution)/shard_map/ppermute | solution.py:31
  197.1 7.4 %collective-permute-start.26 = (f32[3,11,3,128]{3,2,1,0:T(4,128)S(1)}, f32[3,11,3,128]{3,2,1,0:T(4,128)S(1)}, u32[]{:S(2)}, u32[]{:S(2)}) collective-permute-start(f32[3,11,3,128]{3,2,1,0:T(4,128)S(1)} %get-tuple-element.1283), channel_id=1, source_target_pairs={{0,4},{4,8},{8,12},{12,16},{16,20},{20,24},{24,28},{1,5},{5,9},{9,... | collective-permute-start | bytes 152072 | tf_op jit(solution)/shard_map/ppermute | solution.py:29
  204.8 12.5 %collective-permute-start.29 = (f32[3,11,22,3]{3,2,1,0:T(8,128)S(1)}, f32[3,11,22,3]{3,2,1,0:T(8,128)S(1)}, u32[]{:S(2)}, u32[]{:S(2)}) collective-permute-start(f32[3,11,22,3]{3,2,1,0:T(8,128)S(1)} %get-tuple-element.1251), channel_id=1, source_target_pairs={{0,1},{1,2},{2,3},{4,5},{5,6},{6,7},{8,9},{9,10},{10,11},{12,13},{... | collective-permute-start | bytes 26144 | tf_op jit(solution)/shard_map/ppermute | solution.py:29
  207.4 13.2 %collective-permute-start.28 = (f32[3,11,22,3]{3,2,1,0:T(8,128)S(1)}, f32[3,11,22,3]{3,2,1,0:T(8,128)S(1)}, u32[]{:S(2)}, u32[]{:S(2)}) collective-permute-start(f32[3,11,22,3]{3,2,1,0:T(8,128)S(1)} %get-tuple-element.1252), channel_id=1, source_target_pairs={{1,0},{2,1},{3,2},{5,4},{6,5},{7,6},{9,8},{10,9},{11,10},{13,12},{... | collective-permute-start | bytes 26144 | tf_op jit(solution)/shard_map/ppermute | solution.py:31
  242.2 9.2 %collective-permute-start.30 = (f32[3,3,22,134]{3,2,1,0:T(8,128)S(1)}, f32[3,3,22,134]{3,2,1,0:T(8,128)S(1)}, u32[]{:S(2)}, u32[]{:S(2)}) collective-permute-start(f32[3,3,22,134]{3,2,1,0:T(8,128)S(1)} %slice.5737), channel_id=1, source_target_pairs={{0,32},{32,64},{64,96},{96,128},{128,160},{160,192},{192,224},{1,3... | collective-permute-start | bytes 318392 | tf_op jit(solution)/shard_map/ppermute | solution.py:18
  251.5 6.5 %collective-permute-start.32 = (f32[3,8,3,134]{3,2,1,0:T(4,128)S(1)}, f32[3,8,3,134]{3,2,1,0:T(4,128)S(1)}, u32[]{:S(2)}, u32[]{:S(2)}) collective-permute-start(f32[3,8,3,134]{3,2,1,0:T(4,128)S(1)} %get-tuple-element.1207), channel_id=1, source_target_pairs={{4,0},{8,4},{12,8},{16,12},{20,16},{24,20},{28,24},{5,1},{9,5},{13... | collective-permute-start | bytes 115784 | tf_op jit(solution)/shard_map/ppermute | solution.py:18
  254.3 7.4 %collective-permute-start.31 = (f32[3,8,3,134]{3,2,1,0:T(4,128)S(1)}, f32[3,8,3,134]{3,2,1,0:T(4,128)S(1)}, u32[]{:S(2)}, u32[]{:S(2)}) collective-permute-start(f32[3,8,3,134]{3,2,1,0:T(4,128)S(1)} %get-tuple-element.1206), channel_id=1, source_target_pairs={{0,4},{4,8},{8,12},{12,16},{16,20},{20,24},{24,28},{1,5},{5,9},{9,... | collective-permute-start | bytes 115784 | tf_op jit(solution)/shard_map/ppermute | solution.py:18
  261.9 7.6 %collective-permute-start.34 = (f32[3,8,16,3]{3,2,1,0:T(8,128)S(1)}, f32[3,8,16,3]{3,2,1,0:T(8,128)S(1)}, u32[]{:S(2)}, u32[]{:S(2)}) collective-permute-start(f32[3,8,16,3]{3,2,1,0:T(8,128)S(1)} %get-tuple-element.1262), channel_id=1, source_target_pairs={{1,0},{2,1},{3,2},{5,4},{6,5},{7,6},{9,8},{10,9},{11,10},{13,12},{... | collective-permute-start | bytes 13832 | tf_op jit(solution)/shard_map/ppermute | solution.py:18
  265.2 7.6 %collective-permute-start.33 = (f32[3,8,16,3]{3,2,1,0:T(8,128)S(1)}, f32[3,8,16,3]{3,2,1,0:T(8,128)S(1)}, u32[]{:S(2)}, u32[]{:S(2)}) collective-permute-start(f32[3,8,16,3]{3,2,1,0:T(8,128)S(1)} %get-tuple-element.1261), channel_id=1, source_target_pairs={{0,1},{1,2},{2,3},{4,5},{5,6},{6,7},{8,9},{9,10},{10,11},{12,13},{... | collective-permute-start | bytes 13832 | tf_op jit(solution)/shard_map/ppermute | solution.py:18
  (8 other events, 181.8 us)
where the time goes:
time: 278 us; the launch traced here: 274 us
  starting transfers between devices  97.3 us (35%)
  waiting for transfers between devices  92.7 us (33%)
  other arithmetic  77 us (28%)
  local copies, waits for them, and re-layouts  3.58 us (1%)
  between operations  3.35 us (1%)
    ppermute x19, waiting for transfers between devices, shifted(): return lax.ppermute(block, axis, route)  54.8 us
    ppermute x19, starting transfers between devices, shifted(): return lax.ppermute(block, axis, route)  49.8 us
    add x3, other arithmetic, evaluate(): reaction = reaction + place(summed, anchor, full_shape)  32.1 us
    another operation x300, other arithmetic, bond_force(): jnp.stack([factor * radial[0], factor * radial[1], factor * radial[2]])  30.5 us
    ppermute x8, waiting for transfers between devices, with_halo(): lax.ppermute(tail, axis, [(i, (i + 1) % count) for i in range(ends)])  28.5 us
    ppermute x8, starting transfers between devices, with_halo(): lax.ppermute(tail, axis, [(i, (i + 1) % count) for i in range(ends)])  25.3 us
    ppermute x8, starting transfers between devices, with_halo(): lax.ppermute(head, axis, [((i + 1) % count, i) for i in range(ends)])  22.1 us
    ppermute x8, waiting for transfers between devices, with_halo(): lax.ppermute(head, axis, [((i + 1) % count, i) for i in range(ends)])  9.51 us
  transfers between devices with their start and end apart: 35, of which 28 were waited for; matrix products, arithmetic and copies ran while one was open for 3% of the time, Pallas kernels for 0%

commit v1 on v0

v1 whole, which is shorter than its diff:
```python
import functools
import math

import jax
import jax.numpy as jnp
from jax import lax
from jax.experimental import pallas as pl
from jax.experimental.pallas import tpu as pltpu
from jax.sharding import PartitionSpec as P

STEPS = 2
C_BOND = 3.0
DT_STEP = 0.04
REACH = 3
LANES = 128
SLOT = 16
HALF_DT = 0.5 * DT_STEP


def half_offsets():
    result = []
    for step_x in range(0, 4):
        for step_y in range(-3, 4):
            for step_z in range(-3, 4):
                square = step_x * step_x + step_y * step_y + step_z * step_z
                if square == 0 or square > 9:
                    continue
                if step_x > 0 or (step_x == 0 and (step_y > 0 or (step_y == 0 and step_z > 0))):
                    result.append((step_x, step_y, step_z))
    return result


OFFSETS = half_offsets()
BONDS = {step: [] for step in range(-REACH, REACH + 1)}
for _plane, (_a, _b, _c) in enumerate(OFFSETS):
    BONDS[_a].append((_b, _c, _plane, True))
    BONDS[-_a].append((-_b, -_c, _plane, False))


def inner_layers(step, extent):
    return max(0, -step), min(extent, extent - step)


def outer_layers(step, extent):
    return (extent - step, extent) if step > 0 else (0, -step)


def slot_bases(extent, layers_of, steps):
    bases, total = {}, 0
    for step in steps:
        bases[step] = total
        low, high = layers_of(step, extent)
        total += (high - low) * len(BONDS[step])
    return bases, total


STEPS_ALL = list(range(-REACH, REACH + 1))
STEPS_OUT = [step for step in STEPS_ALL if step != 0]


def round_up(count):
    return (count + 7) // 8 * 8


def running(amounts):
    places, total = {}, 0
    for plane, amount in amounts:
        places[plane] = total
        total += amount
    return places, total


Z_UP, Z_UP_COUNT = running([(k, c) for k, (a, b, c) in enumerate(OFFSETS) if c > 0])
Z_DOWN, Z_DOWN_COUNT = running([(k, -c) for k, (a, b, c) in enumerate(OFFSETS) if c < 0])
Y_UP, Y_UP_COUNT = running([(k, b) for k, (a, b, c) in enumerate(OFFSETS) if b > 0])
Y_DOWN, Y_DOWN_COUNT = running([(k, -b) for k, (a, b, c) in enumerate(OFFSETS) if b < 0])
X_UP, X_UP_COUNT = running([(k, a) for k, (a, b, c) in enumerate(OFFSETS) if a > 0])
XY_UP, XY_UP_COUNT = running([(k, a * abs(b)) for k, (a, b, c) in enumerate(OFFSETS) if a * abs(b) > 0])


def lanes_like(value):
    return lax.broadcasted_iota(jnp.int32, value.shape, value.ndim - 1)


def rolled(value, shift):
    shift = shift % LANES
    return value if shift == 0 else pltpu.roll(value, shift, value.ndim - 1)


def beside_columns(low_pack, high_pack, lane_of):
    lanes = lanes_like(low_pack)
    return jnp.where(
        lanes < REACH, rolled(high_pack, -lane_of), rolled(low_pack, LANES - REACH - lane_of)
    )


def moved(main, beside, step):
    if step == 0:
        return main
    lanes = lanes_like(main)
    if step > 0:
        return rolled(jnp.where(lanes < step, beside, main), -step)
    return rolled(jnp.where(lanes >= LANES + step, beside, main), -step)


def pack_columns(field_of, count, extent, height):
    lanes = lax.broadcasted_iota(jnp.int32, (height, LANES), 1)
    up = jnp.zeros((height, LANES), jnp.float32)
    down = up
    for layer in range(extent):
        for field in range(count):
            lane_of = layer * SLOT + field * REACH
            value = field_of(field, layer)
            here = (lanes >= lane_of) & (lanes < lane_of + REACH)
            up = jnp.where(here, rolled(value, lane_of - (LANES - REACH)), up)
            down = jnp.where(here, rolled(value, lane_of), down)
    return up, down


def kept(flag, value):
    return jnp.where(flag > 0, value, 0.0)


def start_kernel(extent, pressure, motion, stiffness, borehole, flags, broken, pore, z_up, z_down, x_up):
    size_x, size_y, _ = extent
    ids = borehole[...]
    level = jnp.zeros(ids.shape, jnp.float32)
    for label in range(pressure.shape[0]):
        level = jnp.where(ids == label, pressure[label], level)
    pore[...] = flags[...].astype(jnp.float32) * level

    def field_of(field, layer):
        if field < 3:
            return motion[field, layer]
        return stiffness[layer] if field == 3 else pore[layer]

    up, down = pack_columns(field_of, 5, size_x, size_y)
    z_up[0:size_y] = up
    z_down[0:size_y] = down

    def one_layer(layer, carry):
        lanes = lax.broadcasted_iota(jnp.int32, (size_y, LANES), 1)
        rows = pl.ds(size_y + layer * size_y, size_y)
        up = jnp.zeros((size_y, LANES), jnp.float32)
        down = up
        for plane, (_, _, c) in enumerate(OFFSETS):
            if c > 0:
                at = Z_UP[plane]
                value = broken[plane, layer].astype(jnp.float32)
                up = jnp.where((lanes >= at) & (lanes < at + c), rolled(value, at + c), up)
            if c < 0:
                at = Z_DOWN[plane]
                value = broken[plane, layer].astype(jnp.float32)
                down = jnp.where((lanes >= at) & (lanes < at - c), rolled(value, at), down)
        z_up[rows] = up
        z_down[rows] = down
        return carry

    lax.fori_loop(0, size_x, one_layer, 0)
    for plane, (a, _, _) in enumerate(OFFSETS):
        for layer in range(a):
            at = (X_UP[plane] + layer) * size_y
            x_up[at : at + size_y] = broken[plane, size_x - a + layer].astype(jnp.float32)


def copy_y_rows(field_of, count, extent, low_pack, high_pack, y_up, y_down):
    size_x, size_y, _ = extent
    for field in range(count):
        for layer in range(size_x):
            at = (field * size_x + layer) * REACH
            y_up[at : at + REACH] = field_of(field, layer, slice(size_y - REACH, size_y))
            y_down[at : at + REACH] = field_of(field, layer, slice(0, REACH))
    at = count * size_x * REACH
    for pack in (low_pack, high_pack):
        y_up[at : at + REACH] = pack[size_y - REACH : size_y]
        y_down[at : at + REACH] = pack[0:REACH]
        at += REACH
    return at


def y_rows_kernel(extent, edges, motion, z_low, z_high, y_up, y_down):
    size_y = extent[1]
    low_pack = kept(edges[0], z_low[0:size_y])
    high_pack = kept(edges[1], z_high[0:size_y])
    copy_y_rows(
        lambda field, layer, rows: motion[field, layer, rows],
        3, extent, low_pack, high_pack, y_up, y_down,
    )


def y_rows_first_kernel(extent, edges, motion, stiffness, pore, broken, z_low, z_high, y_up, y_down):
    size_x, size_y, _ = extent
    low_pack = kept(edges[0], z_low[0:size_y])
    high_pack = kept(edges[1], z_high[0:size_y])

    def field_of(field, layer, rows):
        if field < 3:
            return motion[field, layer, rows]
        return stiffness[layer, rows] if field == 3 else pore[layer, rows]

    base = copy_y_rows(field_of, 5, extent, low_pack, high_pack, y_up, y_down)
    for plane, (_, b, _) in enumerate(OFFSETS):
        for layer in range(size_x):
            if b > 0:
                at = base + Y_UP[plane] * size_x + layer * b
                y_up[at : at + b] = broken[plane, layer, size_y - b : size_y].astype(jnp.float32)
            if b < 0:
                at = base + Y_DOWN[plane] * size_x - layer * b
                y_down[at : at - b] = broken[plane, layer, 0:-b].astype(jnp.float32)
    for order, pack in enumerate((z_low, z_high)):
        for layer in range(size_x):
            first = size_y + layer * size_y
            at = (order * size_x + layer) * REACH
            to_up = base + Y_UP_COUNT * size_x + at
            to_down = base + Y_DOWN_COUNT * size_x + at
            y_up[to_up : to_up + REACH] = pack[first + size_y - REACH : first + size_y]
            y_down[to_down : to_down + REACH] = pack[first : first + REACH]


def widen(target, low_rows, middle, high_rows):
    size_y = middle.shape[0]
    target[0:REACH] = low_rows
    target[REACH : REACH + size_y] = middle
    target[REACH + size_y : 2 * REACH + size_y] = high_rows
    height = target.shape[0]
    target[2 * REACH + size_y : height] = jnp.zeros((height - 2 * REACH - size_y, LANES), jnp.float32)


def widen_fields(edges, field_of, count, extent, z_low, z_high, y_low, y_high, wide, wide_pack):
    size_x, size_y, _ = extent
    for field in range(count):
        for layer in range(size_x):
            at = (field * size_x + layer) * REACH
            widen(
                wide.at[field, layer],
                kept(edges[2], y_low[at : at + REACH]),
                field_of(field, layer),
                kept(edges[3], y_high[at : at + REACH]),
            )
    at = count * size_x * REACH
    for order, pack in enumerate((z_low, z_high)):
        widen(
            wide_pack.at[order],
            kept(edges[2], y_low[at : at + REACH]),
            kept(edges[order], pack[0:size_y]),
            kept(edges[3], y_high[at : at + REACH]),
        )
        at += REACH
    return at


def copy_x_layers(count, size_x, wide, wide_pack, x_up, x_down):
    height = wide.shape[2]
    for field in range(count):
        for layer in range(REACH):
            at = (field * REACH + layer) * height
            x_up[at : at + height] = wide[field, size_x - REACH + layer]
            x_down[at : at + height] = wide[field, layer]
    at = count * REACH * height
    for order in range(2):
        x_up[at : at + height] = wide_pack[order]
        x_down[at : at + height] = wide_pack[order]
        at += height
    return at


def x_layers_kernel(
    extent, edges, motion, z_low, z_high, y_low, y_high, wide, wide_pack, x_up, x_down
):
    widen_fields(
        edges, lambda field, layer: motion[field, layer],
        3, extent, z_low, z_high, y_low, y_high, wide, wide_pack,
    )
    copy_x_layers(3, extent[0], wide, wide_pack, x_up, x_down)


def x_layers_first_kernel(
    extent, edges, motion, stiffness, pore, z_low, z_high, y_low, y_high,
    wide, wide_pack, wide_broken, x_up, x_down,
):
    size_x, size_y, _ = extent

    def field_of(field, layer):
        if field < 3:
            return motion[field, layer]
        return stiffness[layer] if field == 3 else pore[layer]

    base = widen_fields(
        edges, field_of, 5, extent, z_low, z_high, y_low, y_high, wide, wide_pack
    )
    for order, pack in enumerate((z_low, z_high)):
        for layer in range(size_x):
            first = size_y + layer * size_y
            at = (order * size_x + layer) * REACH
            from_low = base + Y_UP_COUNT * size_x + at
            from_high = base + Y_DOWN_COUNT * size_x + at
            widen(
                wide_broken.at[order, layer],
                y_low[from_low : from_low + REACH],
                pack[first : first + size_y],
                y_high[from_high : from_high + REACH],
            )
    at = copy_x_layers(5, size_x, wide, wide_pack, x_up, x_down)
    height = wide.shape[2]
    for order in range(2):
        for layer in range(REACH):
            x_up[at : at + height] = wide_broken[order, size_x - REACH + layer]
            at += height
    for plane, (a, b, _) in enumerate(OFFSETS):
        if a * b == 0:
            continue
        rows, many = abs(b), a * abs(b)
        source = y_low if b > 0 else y_high
        first = base + (Y_UP if b > 0 else Y_DOWN)[plane] * size_x + (size_x - a) * rows
        x_up[at + XY_UP[plane] : at + XY_UP[plane] + many] = source[first : first + many]


def fill_shifts(shifts, place, main, low_pack, high_pack, lane_of, field, add_step):
    beside = beside_columns(low_pack, high_pack, lane_of)
    for step in range(-REACH, REACH + 1):
        value = moved(main, beside, step)
        if add_step and step:
            value = value + float(step)
        shifts[(step + REACH, field) + place] = value


def wanted_keep(low_broken, high_broken, rows_of, plane, step_z):
    value, low, high = rows_of
    if step_z == 0:
        return 1.0 - value
    lanes = lanes_like(value)
    if step_z < 0:
        beside = rolled(low, -Z_UP[plane])
        value = jnp.where(lanes < -step_z, beside, rolled(value, -step_z))
    else:
        beside = rolled(high, LANES - step_z - Z_DOWN[plane])
        value = jnp.where(lanes >= LANES - step_z, beside, rolled(value, -step_z))
    return 1.0 - value


def weights_inner_kernel(
    extent, stiffness, wide, wide_pack, wide_broken, broken, y_low, y_high, weights,
    shifts, planes,
):
    size_x, size_y, _ = extent
    for layer in range(size_x):
        fill_shifts(
            shifts, (layer,), wide[0, layer], wide_pack[0], wide_pack[1],
            layer * SLOT + 3 * REACH, 0, False,
        )
    base = 5 * size_x * REACH + 2 * REACH
    for plane, (_, b, _) in enumerate(OFFSETS):

        def fill(layer, carry, plane=plane):
            planes[plane, layer, REACH : REACH + size_y] = broken[plane, layer].astype(jnp.float32)
            return carry

        lax.fori_loop(0, size_x, fill, 0)
        for layer in range(size_x):
            if b > 0:
                at = base + Y_UP[plane] * size_x + layer * b
                planes[plane, layer, REACH - b : REACH] = y_low[at : at + b]
            if b < 0:
                at = base + Y_DOWN[plane] * size_x - layer * b
                planes[plane, layer, REACH + size_y : REACH + size_y - b] = y_high[at : at - b]
    bases, _ = slot_bases(size_x, inner_layers, STEPS_ALL)
    for step in STEPS_ALL:
        first, last = inner_layers(step, size_x)
        bonds = BONDS[step]

        def one_layer(layer, carry, step=step, first=first, bonds=bonds):
            slot = bases[step] + (layer - first) * len(bonds)
            far_layer = layer + step
            for tile in range(size_y // 8):
                rows = slice(8 * tile, 8 * tile + 8)
                own = stiffness[layer, rows]
                for order, (step_y, step_z, plane, owner) in enumerate(bonds):
                    far_rows = slice(REACH + step_y + 8 * tile, REACH + step_y + 8 * tile + 8)
                    far = shifts[step_z + REACH, 0, far_layer, far_rows]
                    if owner:
                        keep = 1.0 - broken[plane, layer, rows].astype(jnp.float32)
                    else:
                        keep = wanted_keep(
                            None, None,
                            (
                                planes[plane, far_layer, far_rows],
                                wide_broken[0, far_layer, far_rows],
                                wide_broken[1, far_layer, far_rows],
                            ),
                            plane, step_z,
                        )
                    value = keep * (0.5 * C_BOND) * (own + far)
                    weights[slot + order, rows] = jnp.where(far > 0.0, value, 0.0)
            return carry

        lax.fori_loop(first, last, one_layer, 0)


def weights_outer_kernel(
    extent, edges, stiffness, pore, wide, wide_pack, broken, x_broken, x_low, x_high,
    weights, pressing, shifts, planes,
):
    size_x, size_y, _ = extent
    height = wide.shape[2]
    pack_at = 5 * REACH * height
    broken_at = pack_at + 2 * height
    rows_at = broken_at + 2 * REACH * height

    def pack_of(source, order):
        return source[pack_at + order * height : pack_at + (order + 1) * height]

    for side, source in enumerate((x_low, x_high)):
        for layer in range(REACH):
            at = (3 * REACH + layer) * height
            from_layer = size_x - REACH + layer if side == 0 else layer
            fill_shifts(
                shifts, (side * REACH + layer,),
                kept(edges[4 + side], source[at : at + height]),
                kept(edges[4 + side], pack_of(source, 0)),
                kept(edges[4 + side], pack_of(source, 1)),
                from_layer * SLOT + 3 * REACH, 0, False,
            )
    for plane, (a, b, _) in enumerate(OFFSETS):
        for layer in range(a):
            at = (X_UP[plane] + layer) * size_y
            place = X_UP[plane] + layer
            planes[place, REACH : REACH + size_y] = x_broken[at : at + size_y]
            at = rows_at + XY_UP.get(plane, 0) + layer * abs(b)
            if b > 0:
                planes[place, REACH - b : REACH] = x_low[at : at + b]
            if b < 0:
                planes[place, REACH + size_y : REACH + size_y - b] = x_low[at : at - b]
    bases, _ = slot_bases(size_x, outer_layers, STEPS_OUT)
    for step in STEPS_OUT:
        first, last = outer_layers(step, size_x)
        bonds = BONDS[step]
        for layer in range(first, last):
            slot = bases[step] + (layer - first) * len(bonds)
            far_layer = layer + step
            far_layer = far_layer + REACH if far_layer < 0 else far_layer - size_x + REACH
            for tile in range(size_y // 8):
                rows = slice(8 * tile, 8 * tile + 8)
                own = stiffness[layer, rows]
                for order, (step_y, step_z, plane, owner) in enumerate(bonds):
                    far_rows = slice(REACH + step_y + 8 * tile, REACH + step_y + 8 * tile + 8)
                    far = shifts[step_z + REACH, 0, far_layer, far_rows]
                    if owner:
                        keep = 1.0 - broken[plane, layer, rows].astype(jnp.float32)
                    else:
                        low_at = broken_at + far_layer * height
                        high_at = low_at + REACH * height
                        moved_rows = slice(far_rows.start + low_at, far_rows.stop + low_at)
                        moved_high = slice(far_rows.start + high_at, far_rows.stop + high_at)
                        keep = wanted_keep(
                            None, None,
                            (
                                planes[X_UP[plane] + layer, far_rows],
                                x_low[moved_rows],
                                x_low[moved_high],
                            ),
                            plane, step_z,
                        )
                    value = keep * (0.5 * C_BOND) * (own + far)
                    weights[slot + order, rows] = jnp.where(far > 0.0, value, 0.0)

    middle = slice(REACH, REACH + size_y)

    def wide_field(field, layer):
        if layer < 0 or layer >= size_x:
            source = x_low if layer < 0 else x_high
            at = (field * REACH + (layer + REACH if layer < 0 else layer - size_x)) * height
            return kept(edges[4 if layer < 0 else 5], source[at : at + height])
        return wide[field - 3, layer]

    for layer in range(size_x):
        own = pore[layer]
        for axis in range(3):
            total = jnp.zeros((size_y, LANES), jnp.float32)
            for sign in (1, -1):
                if axis == 0:
                    inside = wide_field(3, layer + sign)[middle]
                    level = wide_field(4, layer + sign)[middle]
                elif axis == 1:
                    rows = slice(REACH + sign, REACH + sign + size_y)
                    inside = wide[0, layer, rows]
                    level = wide[1, layer, rows]
                else:
                    inside, level = (
                        moved(
                            wide[field - 3, layer],
                            beside_columns(
                                wide_pack[0], wide_pack[1], layer * SLOT + field * REACH
                            ),
                            sign,
                        )[middle]
                        for field in (3, 4)
                    )
                total = total + jnp.where(inside > 0.0, (-0.5 * sign) * (level - own), 0.0)
            pressing[axis, layer] = total


def add_bonds(extent, step, layer, far_layer, motion, shifts, weights, slot, total):
    size_y = extent[1]
    for tile in range(size_y // 8):
        rows = slice(8 * tile, 8 * tile + 8)
        own = [motion[axis, layer, rows] for axis in range(3)]
        near_x = own[0] - float(step)
        near_y = {step_y: own[1] - float(step_y) for step_y in range(-REACH, REACH + 1)}
        force = [total[axis, layer, rows] for axis in range(3)]
        for order, (step_y, step_z, plane, _) in enumerate(BONDS[step]):
            far_rows = slice(REACH + step_y + 8 * tile, REACH + step_y + 8 * tile + 8)
            far = [shifts[step_z + REACH, axis, far_layer, far_rows] for axis in range(3)]
            radial = [far[0] - near_x, far[1] - near_y[step_y], far[2] - own[2]]
            square = radial[0] * radial[0] + radial[1] * radial[1] + radial[2] * radial[2]
            rest = math.sqrt(sum(part * part for part in OFFSETS[plane]))
            factor = weights[slot + order, rows] * (1.0 / rest - lax.rsqrt(square))
            force = [force[axis] + factor * radial[axis] for axis in range(3)]
        for axis in range(3):
            total[axis, layer, rows] = force[axis]


def force_inner_kernel(extent, motion, wide, wide_pack, weights, total, shifts):
    size_x = extent[0]
    total[...] = jnp.zeros(total.shape, jnp.float32)
    for layer in range(size_x):
        for axis in range(3):
            fill_shifts(
                shifts, (layer,), wide[axis, layer], wide_pack[0], wide_pack[1],
                layer * SLOT + axis * REACH, axis, axis == 2,
            )
    bases, _ = slot_bases(size_x, inner_layers, STEPS_ALL)
    for step in STEPS_ALL:
        first, last = inner_layers(step, size_x)

        def one_layer(layer, carry, step=step, first=first):
            slot = bases[step] + (layer - first) * len(BONDS[step])
            add_bonds(extent, step, layer, layer + step, motion, shifts, weights, slot, total)
            return carry

        lax.fori_loop(first, last, one_layer, 0)


def finish_kernel(extent, count, stage, edges, motion, speed, pressing, inner, weights, x_low, x_high, *refs):
    size_x, size_y, _ = extent
    if stage == "last":
        accel_out, speed_out, total, shifts = refs
    else:
        motion_out, speed_out, z_up, z_down, total, shifts = refs
    height = (x_low.shape[0] if stage != "first" else x_high.shape[0]) // (count * REACH + 2)
    total[...] = inner[...] + pressing[...]
    pack_at = count * REACH * height
    for side, source in enumerate((x_low, x_high)):
        packs = [
            kept(edges[4 + side], source[pack_at + order * height : pack_at + (order + 1) * height])
            for order in range(2)
        ]
        for layer in range(REACH):
            from_layer = size_x - REACH + layer if side == 0 else layer
            for axis in range(3):
                at = (axis * REACH + layer) * height
                fill_shifts(
                    shifts, (side * REACH + layer,),
                    kept(edges[4 + side], source[at : at + height]),
                    packs[0], packs[1], from_layer * SLOT + axis * REACH, axis, axis == 2,
                )
    bases, _ = slot_bases(size_x, outer_layers, STEPS_OUT)
    for step in STEPS_OUT:
        first, last = outer_layers(step, size_x)

        def one_layer(layer, carry, step=step, first=first):
            slot = bases[step] + (layer - first) * len(BONDS[step])
            far_layer = layer + step + (REACH if step < 0 else REACH - size_x)
            add_bonds(extent, step, layer, far_layer, motion, shifts, weights, slot, total)
            return carry

        lax.fori_loop(first, last, one_layer, 0)
    accel = total[...]
    new_speed = speed[...] + HALF_DT * accel
    if stage == "last":
        accel_out[...] = accel
        speed_out[...] = new_speed
        return
    if stage == "middle":
        new_speed = new_speed + HALF_DT * accel
    speed_out[...] = new_speed
    motion_out[...] = motion[...] + DT_STEP * new_speed
    up, down = pack_columns(lambda axis, layer: motion_out[axis, layer], 3, size_x, size_y)
    z_up[...] = up
    z_down[...] = down


VMEM = pl.BlockSpec(memory_space=pltpu.VMEM)
SMEM = pl.BlockSpec(memory_space=pltpu.SMEM)


def call(kernel, scalars, operands, shapes, scratch=(), name=None):
    return pl.pallas_call(
        kernel,
        out_shape=[jax.ShapeDtypeStruct(shape, jnp.float32) for shape in shapes],
        in_specs=[SMEM] * len(scalars) + [VMEM] * len(operands),
        out_specs=[VMEM] * len(shapes),
        scratch_shapes=[pltpu.VMEM(shape, jnp.float32) for shape in scratch],
        compiler_params=pltpu.CompilerParams(vmem_limit_bytes=56 * 1024 * 1024),
        name=name,
    )(*scalars, *operands)


def sent(value, axis, distance):
    count = lax.axis_size(axis)
    return lax.ppermute(value, axis, [(i, (i + distance) % count) for i in range(count)])


def on_device(displacement, velocity, stiffness, broken, borehole_id, flags, pressure):
    extent = stiffness.shape
    size_x, size_y, _ = extent
    height = size_y + 8
    edges = jnp.stack(
        [
            end
            for axis in ("gz", "gy", "gx")
            for end in (
                (lax.axis_index(axis) > 0).astype(jnp.int32),
                (lax.axis_index(axis) < lax.axis_size(axis) - 1).astype(jnp.int32),
            )
        ]
    )
    field = (size_x, size_y, LANES)
    vector = (3,) + field
    part = functools.partial

    pack = (size_y + size_x * size_y, LANES)
    pore, z_up, z_down, x_up = call(
        part(start_kernel, extent), [pressure],
        [displacement, stiffness, borehole_id, flags, broken],
        [field, pack, pack, (X_UP_COUNT * size_y, LANES)], name="start",
    )
    z_low = sent(z_up, "gz", 1)
    z_high = sent(z_down, "gz", -1)
    x_broken = sent(x_up, "gx", 1)
    base = 5 * size_x * REACH + 2 * REACH + 2 * size_x * REACH
    y_up, y_down = call(
        part(y_rows_first_kernel, extent), [edges],
        [displacement, stiffness, pore, broken, z_low, z_high],
        [
            (round_up(base + Y_UP_COUNT * size_x), LANES),
            (round_up(base + Y_DOWN_COUNT * size_x), LANES),
        ], name="y_rows_first",
    )
    y_low = sent(y_up, "gy", 1)
    y_high = sent(y_down, "gy", -1)
    layers = (5 * REACH + 2) * height
    wide, wide_pack, wide_broken, x_up, x_down = call(
        part(x_layers_first_kernel, extent), [edges],
        [displacement, stiffness, pore, z_low, z_high, y_low, y_high],
        [
            (5, size_x, height, LANES),
            (2, height, LANES),
            (2, size_x, height, LANES),
            (round_up(layers + 2 * REACH * height + XY_UP_COUNT), LANES),
            (layers, LANES),
        ], name="x_layers_first",
    )
    x_low = sent(x_up, "gx", 1)
    x_high = sent(x_down, "gx", -1)
    moves = 2 * REACH + 1
    inner_slots = slot_bases(size_x, inner_layers, STEPS_ALL)[1]
    outer_slots = slot_bases(size_x, outer_layers, STEPS_OUT)[1]
    (inner_weights,) = call(
        part(weights_inner_kernel, extent), [],
        [stiffness, wide[3:], wide_pack, wide_broken, broken, y_low, y_high],
        [(inner_slots, size_y, LANES)],
        [(moves, 1, size_x, height, LANES), (len(OFFSETS), size_x, height, LANES)],
        name="weights_inner",
    )

    def inner_force(motion, wide, wide_pack):
        return call(
            part(force_inner_kernel, extent), [], [motion, wide, wide_pack, inner_weights],
            [vector], [(moves, 3, size_x, height, LANES)], name="force_inner",
        )[0]

    inner = inner_force(displacement, wide[:3], wide_pack)
    outer_weights, pressing = call(
        part(weights_outer_kernel, extent), [edges],
        [stiffness, pore, wide[3:], wide_pack, broken, x_broken, x_low, x_high],
        [(outer_slots, size_y, LANES), vector],
        [(moves, 1, 2 * REACH, height, LANES), (X_UP_COUNT, height, LANES)],
        name="weights_outer",
    )

    def finish(stage, count, motion, speed, inner, x_low, x_high):
        columns = (size_y, LANES)
        shapes = [vector, vector] if stage == "last" else [vector, vector, columns, columns]
        return call(
            part(finish_kernel, extent, count, stage), [edges],
            [motion, speed, pressing, inner, outer_weights, x_low, x_high],
            shapes, [vector, (moves, 3, 2 * REACH, height, LANES)], name="finish_" + stage,
        )

    motion, speed, z_up, z_down = finish(
        "first", 5, displacement, velocity, inner, x_low, x_high
    )
    for step_index in range(STEPS):
        z_low = sent(z_up, "gz", 1)
        z_high = sent(z_down, "gz", -1)
        rows = (round_up(3 * size_x * REACH + 2 * REACH), LANES)
        y_up, y_down = call(
            part(y_rows_kernel, extent), [edges], [motion, z_low, z_high], [rows, rows],
            name="y_rows",
        )
        y_low = sent(y_up, "gy", 1)
        y_high = sent(y_down, "gy", -1)
        layers = (3 * REACH + 2) * height
        wide, wide_pack, x_up, x_down = call(
            part(x_layers_kernel, extent), [edges],
            [motion, z_low, z_high, y_low, y_high],
            [
                (3, size_x, height, LANES),
                (2, height, LANES),
                (layers, LANES),
                (layers, LANES),
            ], name="x_layers",
        )
        x_low = sent(x_up, "gx", 1)
        x_high = sent(x_down, "gx", -1)
        inner = inner_force(motion, wide, wide_pack)
        if step_index < STEPS - 1:
            motion, speed, z_up, z_down = finish("middle", 3, motion, speed, inner, x_low, x_high)
        else:
            accel, speed = finish("last", 3, motion, speed, inner, x_low, x_high)
    return (motion, speed, accel)


def solution(mesh):
    in_specs = (
        P(None, "gx", "gy", "gz"),
        P(None, "gx", "gy", "gz"),
        P("gx", "gy", "gz"),
        P(None, "gx", "gy", "gz"),
        P("gx", "gy", "gz"),
        P("gx", "gy", "gz"),
        P(),
    )
    out_specs = (P(None, "gx", "gy", "gz"), P(None, "gx", "gy", "gz"), P(None, "gx", "gy", "gz"))
    return jax.shard_map(
        on_device, mesh=mesh, in_specs=in_specs, out_specs=out_specs, check_vma=False
    )
```

time: 278 us -> 164 us (0.59)
  the two profiles are of different devices: /device:TPU:92 before, /device:TPU:6 now
where the time goes in v1:
time: 164 us
  Pallas kernels  81.7 us (50%)
  starting transfers between devices  37.1 us (23%)
  waiting for transfers between devices  32.3 us (20%)
  local copies, waits for them, and re-layouts  11.6 us (7%)
    pallas_call x15, Pallas kernels, call(): pl.pallas_call(kernel, out_shape=[jax.ShapeDtypeStruct(shape, jnp.float32...  81.7 us
    ppermute x19, starting transfers between devices, sent(): lax.ppermute(value, axis, [(i, (i + distance) % count) for i in range(cou...  37.1 us
    ppermute x19, waiting for transfers between devices, sent(): lax.ppermute(value, axis, [(i, (i + distance) % count) for i in range(cou...  32.3 us
    unnamed x40, local copies, waits for them, and re-layouts  8.16 us
  transfers between devices with their start and end apart: 19, of which 10 were waited for; matrix products, arithmetic and copies ran while one was open for 2% of the time, Pallas kernels for 29%

profile of v1, /device:TPU:6, one launch (start us, length us, event | category | flops | bytes accessed | tf_op | source)
XLA Modules:
  0.0 163.8 jit_solution(12120996055722067347)
XLA Ops:
  0.6 4.8 %start.1 = (f32[8,16,128]{2,1,0:T(8,128)}, f32[144,128]{1,0:T(8,128)}, f32[144,128]{1,0:T(8,128)}, f32[1120,128]{1,0:T(8,128)}) custom-call(f32[8]{0:T(128)} %pressure.1, f32[3,8,16,128]{3,2,1,0:T(8,128)} %motion.9, f32[8,16,128]{2,1,0:T(8,128)} %stiffness.9, s32[8,16,128]{2,1,0:T(8,128)} %borehole.1, s32[8,16,128]{2,1,0:T(8,128)} %flags.1, ...), custom_call_target="tpu_custom_call" | custom-call | tf_op jit(solution)/shard_map/start/pallas_call | solution.py:597
  5.4 2.2 %collective-permute-start = (f32[144,128]{1,0:T(8,128)}, f32[144,128]{1,0:T(8,128)S(1)}, u32[]{:S(2)}, u32[]{:S(2)}) collective-permute-start(f32[144,128]{1,0:T(8,128)} %get-tuple-element.39), channel_id=1, source_target_pairs={{0,1},{1,2},{2,3},{3,0},{4,5},{5,6},{6,7},{7,4},{8,9},{9,10},{10,1... | collective-permute-start | bytes 221192 | tf_op jit(solution)/shard_map/ppermute | solution.py:610
  8.2 1.8 %collective-permute-done.z_low = f32[144,128]{1,0:T(8,128)S(1)} collective-permute-done((f32[144,128]{1,0:T(8,128)}, f32[144,128]{1,0:T(8,128)S(1)}, u32[]{:S(2)}, u32[]{:S(2)}) %collective-permute-start) | collective-permute-done | bytes 73760 | tf_op jit(solution)/shard_map/ppermute | solution.py:610
  10.0 3.4 %collective-permute-done.1.z_high = f32[144,128]{1,0:T(8,128)S(1)} collective-permute-done((f32[144,128]{1,0:T(8,128)}, f32[144,128]{1,0:T(8,128)S(1)}, u32[]{:S(2)}, u32[]{:S(2)}) %collective-permute-start.1) | collective-permute-done | bytes 73760 | tf_op jit(solution)/shard_map/ppermute | solution.py:610
  14.0 3.2 %y_rows_first.1 = (f32[528,128]{1,0:T(8,128)}, f32[384,128]{1,0:T(8,128)}) custom-call(s32[6]{0:T(128)} %stack.36.edges, f32[3,8,16,128]{3,2,1,0:T(8,128)} %motion.9, f32[8,16,128]{2,1,0:T(8,128)} %stiffness.9, f32[8,16,128]{2,1,0:T(8,128)} %get-tuple-element.38.pore, s32[61,8,16,128]{3,2,1,0:T(8,128)} %broken.7, f32[144,128]{1,0:T(8,128)} %copy-done.5, ...), custom_call_target="tpu_custom_call" | custom-call | tf_op jit(solution)/shard_map/y_rows_first/pallas_call | solution.py:597
  17.4 4.0 %collective-permute-start.3 = (f32[384,128]{1,0:T(8,128)}, f32[384,128]{1,0:T(8,128)S(1)}, u32[]{:S(2)}, u32[]{:S(2)}) collective-permute-start(f32[384,128]{1,0:T(8,128)} %get-tuple-element.42), channel_id=1, source_target_pairs={{0,28},{4,0},{8,4},{12,8},{16,12},{20,16},{24,20},{28,24},{1,29},{... | collective-permute-start | bytes 589832 | tf_op jit(solution)/shard_map/ppermute | solution.py:610
  21.4 11.7 %collective-permute-done.3.y_high = f32[384,128]{1,0:T(8,128)S(1)} collective-permute-done((f32[384,128]{1,0:T(8,128)}, f32[384,128]{1,0:T(8,128)S(1)}, u32[]{:S(2)}, u32[]{:S(2)}) %collective-permute-start.3) | collective-permute-done | bytes 196640 | tf_op jit(solution)/shard_map/ppermute | solution.py:610
  34.5 2.3 %x_layers_first.1 = (f32[5,8,24,128]{3,2,1,0:T(8,128)}, f32[2,24,128]{2,1,0:T(8,128)}, f32[2,8,24,128]{3,2,1,0:T(8,128)}, f32[632,128]{1,0:T(8,128)}, f32[408,128]{1,0:T(8,128)}) custom-call(s32[6]{0:T(128)} %stack.36.edges, f32[3,8,16,128]{3,2,1,0:T(8,128)} %motion.9, f32[8,16,128]{2,1,0:T(8,128)} %stiffness.9, f32[8,16,128]{2,1,0:T(8,128)} %get-tuple-element.38.pore, ...), custom_call_target="tpu_custom_call" | custom-call | tf_op jit(solution)/shard_map/x_layers_first/pallas_call | solution.py:597
  36.8 5.6 %collective-permute-start.5 = (f32[632,128]{1,0:T(8,128)}, f32[632,128]{1,0:T(8,128)S(1)}, u32[]{:S(2)}, u32[]{:S(2)}) collective-permute-start(f32[632,128]{1,0:T(8,128)} %get-tuple-element.46), channel_id=1, source_target_pairs={{0,32},{32,64},{64,96},{96,128},{128,160},{160,192},{192,224},{224... | collective-permute-start | bytes 970760 | tf_op jit(solution)/shard_map/ppermute | solution.py:610
  42.4 5.0 %collective-permute-start.6 = (f32[408,128]{1,0:T(8,128)}, f32[408,128]{1,0:T(8,128)S(1)}, u32[]{:S(2)}, u32[]{:S(2)}) collective-permute-start(f32[408,128]{1,0:T(8,128)} %get-tuple-element.47), channel_id=1, source_target_pairs={{0,224},{32,0},{64,32},{96,64},{128,96},{160,128},{192,160},{224,1... | collective-permute-start | bytes 626696 | tf_op jit(solution)/shard_map/ppermute | solution.py:610
  49.1 1.7 %slice.8.wide = f32[3,8,24,128]{3,2,1,0:T(8,128)} slice(f32[5,8,24,128]{3,2,1,0:T(8,128)} %get-tuple-element.43), slice={[0:3], [0:8], [0:24], [0:128]} | slice | bytes 589824 | tf_op jit(solution)/shard_map/slice | solution.py:682
  50.7 12.3 %weights_inner.1.weights = f32[836,16,128]{2,1,0:T(8,128)} custom-call(f32[8,16,128]{2,1,0:T(8,128)} %stiffness.9, f32[2,8,24,128]{3,2,1,0:T(8,128)} %slice.7.wide, f32[2,24,128]{2,1,0:T(8,128)} %get-tuple-element.44.wide_pack, f32[2,8,24,128]{3,2,1,0:T(8,128)} %get-tuple-element.49.wide_broken, s32[61,8,16,128]{3,2,1,0:T(8,128)} %broken.7, ...), custom_call_target="tpu_custom_call" | custom-call | tf_op jit(solution)/shard_map/weights_inner/pallas_call | solution.py:597
  63.1 10.9 %force_inner.3.inner = f32[3,8,16,128]{3,2,1,0:T(8,128)} custom-call(f32[3,8,16,128]{3,2,1,0:T(8,128)} %motion.9, f32[3,8,24,128]{3,2,1,0:T(8,128)} %slice.8.wide, f32[2,24,128]{2,1,0:T(8,128)} %get-tuple-element.44.wide_pack, f32[836,16,128]{2,1,0:T(8,128)} %weights_inner.1.weights), custom_call_target="tpu_custom_call" | custom-call | tf_op jit(solution)/shard_map/force_inner/pallas_call | solution.py:597
  75.7 5.3 %weights_outer.1 = (f32[140,16,128]{2,1,0:T(8,128)}, f32[3,8,16,128]{3,2,1,0:T(8,128)}) custom-call(s32[6]{0:T(128)} %stack.36.edges, f32[8,16,128]{2,1,0:T(8,128)} %stiffness.9, f32[8,16,128]{2,1,0:T(8,128)} %get-tuple-element.38.pore, f32[2,8,24,128]{3,2,1,0:T(8,128)} %slice.7.wide, f32[2,24,128]{2,1,0:T(8,128)} %get-tuple-element.44.wide_pack, ...), custom_call_target="tpu_custom_call" | custom-call | tf_op jit(solution)/shard_map/weights_outer/pallas_call | solution.py:597
  81.0 4.7 %finish_first.1 = (f32[3,8,16,128]{3,2,1,0:T(8,128)}, f32[3,8,16,128]{3,2,1,0:T(8,128)}, f32[16,128]{1,0:T(8,128)}, f32[16,128]{1,0:T(8,128)}) custom-call(s32[6]{0:T(128)} %stack.36.edges, f32[3,8,16,128]{3,2,1,0:T(8,128)} %motion.9, f32[3,8,16,128]{3,2,1,0:T(8,128)} %speed.1, f32[3,8,16,128]{3,2,1,0:T(8,128)} %get-tuple-element.48.pressing, ...), custom_call_target="tpu_custom_call" | custom-call | tf_op jit(solution)/shard_map/finish_first/pallas_call | solution.py:597
  86.0 1.7 %collective-permute-start.8 = (f32[16,128]{1,0:T(8,128)}, f32[16,128]{1,0:T(8,128)S(1)}, u32[]{:S(2)}, u32[]{:S(2)}) collective-permute-start(f32[16,128]{1,0:T(8,128)} %get-tuple-element.54), channel_id=1, source_target_pairs={{0,3},{1,0},{2,1},{3,2},{4,7},{5,4},{6,5},{7,6},{8,11},{9,8},{10,9... | collective-permute-start | bytes 24584 | tf_op jit(solution)/shard_map/ppermute | solution.py:610
  87.7 1.8 %collective-permute-done.7.z_low = f32[16,128]{1,0:T(8,128)S(1)} collective-permute-done((f32[16,128]{1,0:T(8,128)}, f32[16,128]{1,0:T(8,128)S(1)}, u32[]{:S(2)}, u32[]{:S(2)}) %collective-permute-start.7) | collective-permute-done | bytes 8224 | tf_op jit(solution)/shard_map/ppermute | solution.py:610
  93.3 4.2 %collective-permute-start.10 = (f32[80,128]{1,0:T(8,128)}, f32[80,128]{1,0:T(8,128)S(1)}, u32[]{:S(2)}, u32[]{:S(2)}) collective-permute-start(f32[80,128]{1,0:T(8,128)} %get-tuple-element.56), channel_id=1, source_target_pairs={{0,28},{4,0},{8,4},{12,8},{16,12},{20,16},{24,20},{28,24},{1,29},{... | collective-permute-start | bytes 122888 | tf_op jit(solution)/shard_map/ppermute | solution.py:610
  97.5 2.0 %collective-permute-done.10.y_high = f32[80,128]{1,0:T(8,128)S(1)} collective-permute-done((f32[80,128]{1,0:T(8,128)}, f32[80,128]{1,0:T(8,128)S(1)}, u32[]{:S(2)}, u32[]{:S(2)}) %collective-permute-start.10) | collective-permute-done | bytes 40992 | tf_op jit(solution)/shard_map/ppermute | solution.py:610
  99.5 4.3 %collective-permute-done.9.y_low = f32[80,128]{1,0:T(8,128)S(1)} collective-permute-done((f32[80,128]{1,0:T(8,128)}, f32[80,128]{1,0:T(8,128)S(1)}, u32[]{:S(2)}, u32[]{:S(2)}) %collective-permute-start.9) | collective-permute-done | bytes 40992 | tf_op jit(solution)/shard_map/ppermute | solution.py:610
  104.4 1.8 %x_layers.2 = (f32[3,8,24,128]{3,2,1,0:T(8,128)}, f32[2,24,128]{2,1,0:T(8,128)}, f32[264,128]{1,0:T(8,128)}, f32[264,128]{1,0:T(8,128)}) custom-call(s32[6]{0:T(128)} %stack.36.edges, f32[3,8,16,128]{3,2,1,0:T(8,128)} %get-tuple-element.51.motion, f32[16,128]{1,0:T(8,128)} %copy-done.15, f32[16,128]{1,0:T(8,128)} %copy-done.17, f32[80,128]{1,0:T(8,128)} %copy-done.13, ...), custom_call_target="tpu_custom_call" | custom-call | tf_op jit(solution)/shard_map/x_layers/pallas_call | solution.py:597
  106.3 3.9 %collective-permute-start.12 = (f32[264,128]{1,0:T(8,128)}, f32[264,128]{1,0:T(8,128)S(1)}, u32[]{:S(2)}, u32[]{:S(2)}) collective-permute-start(f32[264,128]{1,0:T(8,128)} %get-tuple-element.60), channel_id=1, source_target_pairs={{0,224},{32,0},{64,32},{96,64},{128,96},{160,128},{192,160},{224,1... | collective-permute-start | bytes 405512 | tf_op jit(solution)/shard_map/ppermute | solution.py:610
  110.1 10.9 %force_inner.4.inner = f32[3,8,16,128]{3,2,1,0:T(8,128)} custom-call(f32[3,8,16,128]{3,2,1,0:T(8,128)} %get-tuple-element.51.motion, f32[3,8,24,128]{3,2,1,0:T(8,128)} %get-tuple-element.57.wide, f32[2,24,128]{2,1,0:T(8,128)} %get-tuple-element.58.wide_pack, f32[836,16,128]{2,1,0:T(8,128)} %weights_inner.1.weights), custom_call_target="tpu_custom_call" | custom-call | tf_op jit(solution)/shard_map/force_inner/pallas_call | solution.py:597
  121.7 4.7 %finish_middle.1 = (f32[3,8,16,128]{3,2,1,0:T(8,128)}, f32[3,8,16,128]{3,2,1,0:T(8,128)}, f32[16,128]{1,0:T(8,128)}, f32[16,128]{1,0:T(8,128)}) custom-call(s32[6]{0:T(128)} %stack.36.edges, f32[3,8,16,128]{3,2,1,0:T(8,128)} %get-tuple-element.51.motion, f32[3,8,16,128]{3,2,1,0:T(8,128)} %get-tuple-element.52.speed, ...), custom_call_target="tpu_custom_call" | custom-call | tf_op jit(solution)/shard_map/finish_middle/pallas_call | solution.py:597
  128.5 1.8 %collective-permute-done.13.z_low = f32[16,128]{1,0:T(8,128)S(1)} collective-permute-done((f32[16,128]{1,0:T(8,128)}, f32[16,128]{1,0:T(8,128)S(1)}, u32[]{:S(2)}, u32[]{:S(2)}) %collective-permute-start.13) | collective-permute-done | bytes 8224 | tf_op jit(solution)/shard_map/ppermute | solution.py:610
  130.3 1.7 %collective-permute-done.14.z_high = f32[16,128]{1,0:T(8,128)S(1)} collective-permute-done((f32[16,128]{1,0:T(8,128)}, f32[16,128]{1,0:T(8,128)S(1)}, u32[]{:S(2)}, u32[]{:S(2)}) %collective-permute-start.14) | collective-permute-done | bytes 8224 | tf_op jit(solution)/shard_map/ppermute | solution.py:610
  134.2 4.1 %collective-permute-start.16 = (f32[80,128]{1,0:T(8,128)}, f32[80,128]{1,0:T(8,128)S(1)}, u32[]{:S(2)}, u32[]{:S(2)}) collective-permute-start(f32[80,128]{1,0:T(8,128)} %get-tuple-element.66), channel_id=1, source_target_pairs={{0,28},{4,0},{8,4},{12,8},{16,12},{20,16},{24,20},{28,24},{1,29},{... | collective-permute-start | bytes 122888 | tf_op jit(solution)/shard_map/ppermute | solution.py:610
  138.3 2.2 %collective-permute-done.15.y_low = f32[80,128]{1,0:T(8,128)S(1)} collective-permute-done((f32[80,128]{1,0:T(8,128)}, f32[80,128]{1,0:T(8,128)S(1)}, u32[]{:S(2)}, u32[]{:S(2)}) %collective-permute-start.15) | collective-permute-done | bytes 40992 | tf_op jit(solution)/shard_map/ppermute | solution.py:610
  141.8 1.8 %x_layers.3 = (f32[3,8,24,128]{3,2,1,0:T(8,128)}, f32[2,24,128]{2,1,0:T(8,128)}, f32[264,128]{1,0:T(8,128)}, f32[264,128]{1,0:T(8,128)}) custom-call(s32[6]{0:T(128)} %stack.36.edges, f32[3,8,16,128]{3,2,1,0:T(8,128)} %get-tuple-element.35.motion, f32[16,128]{1,0:T(8,128)} %copy-done.16, f32[16,128]{1,0:T(8,128)} %copy-done.18, f32[80,128]{1,0:T(8,128)} %copy-done.12, ...), custom_call_target="tpu_custom_call" | custom-call | tf_op jit(solution)/shard_map/x_layers/pallas_call | solution.py:597
  143.6 3.9 %collective-permute-start.18 = (f32[264,128]{1,0:T(8,128)}, f32[264,128]{1,0:T(8,128)S(1)}, u32[]{:S(2)}, u32[]{:S(2)}) collective-permute-start(f32[264,128]{1,0:T(8,128)} %get-tuple-element.70), channel_id=1, source_target_pairs={{0,224},{32,0},{64,32},{96,64},{128,96},{160,128},{192,160},{224,1... | collective-permute-start | bytes 405512 | tf_op jit(solution)/shard_map/ppermute | solution.py:610
  147.4 10.9 %force_inner.5.inner = f32[3,8,16,128]{3,2,1,0:T(8,128)} custom-call(f32[3,8,16,128]{3,2,1,0:T(8,128)} %get-tuple-element.35.motion, f32[3,8,24,128]{3,2,1,0:T(8,128)} %get-tuple-element.67.wide, f32[2,24,128]{2,1,0:T(8,128)} %get-tuple-element.68.wide_pack, f32[836,16,128]{2,1,0:T(8,128)} %weights_inner.1.weights), custom_call_target="tpu_custom_call" | custom-call | tf_op jit(solution)/shard_map/force_inner/pallas_call | solution.py:597
  159.1 4.7 %finish_last.1 = (f32[3,8,16,128]{3,2,1,0:T(8,128)}, f32[3,8,16,128]{3,2,1,0:T(8,128)}) custom-call(s32[6]{0:T(128)} %stack.36.edges, f32[3,8,16,128]{3,2,1,0:T(8,128)} %get-tuple-element.35.motion, f32[3,8,16,128]{3,2,1,0:T(8,128)} %get-tuple-element.62.speed, f32[3,8,16,128]{3,2,1,0:T(8,128)} %get-tuple-element.48.pressing, ...), custom_call_target="tpu_custom_call" | custom-call | tf_op jit(solution)/shard_map/finish_last/pallas_call | solution.py:597
  (65 shorter events, 17.6 us)
Async XLA Ops:
  5.4 12.0 %copy-start.19 = (f32[1120,128]{1,0:T(8,128)S(1)}, f32[1120,128]{1,0:T(8,128)}, u32[]{:S(2)}) copy-start(f32[1120,128]{1,0:T(8,128)} %get-tuple-element.45) | copy-start | bytes 1720324
  5.4 4.6 %collective-permute-start = (f32[144,128]{1,0:T(8,128)}, f32[144,128]{1,0:T(8,128)S(1)}, u32[]{:S(2)}, u32[]{:S(2)}) collective-permute-start(f32[144,128]{1,0:T(8,128)} %get-tuple-element.39), channel_id=1, source_target_pairs={{0,1},{1,2},{2,3},{3,0},{4,5},{5,6},{6,7},{7,4},{8,9},{9,10},{10,1... | collective-permute-start | bytes 221192 | tf_op jit(solution)/shard_map/ppermute | solution.py:610
  7.6 5.8 %collective-permute-start.1 = (f32[144,128]{1,0:T(8,128)}, f32[144,128]{1,0:T(8,128)S(1)}, u32[]{:S(2)}, u32[]{:S(2)}) collective-permute-start(f32[144,128]{1,0:T(8,128)} %get-tuple-element.40), channel_id=1, source_target_pairs={{0,3},{1,0},{2,1},{3,2},{4,7},{5,4},{6,5},{7,6},{8,11},{9,8},{10,9... | collective-permute-start | bytes 221192 | tf_op jit(solution)/shard_map/ppermute | solution.py:610
  10.0 3.4 %copy-start.5 = (f32[144,128]{1,0:T(8,128)}, f32[144,128]{1,0:T(8,128)S(1)}, u32[]{:S(2)}) copy-start(f32[144,128]{1,0:T(8,128)S(1)} %collective-permute-done.z_low) | copy-start | bytes 221188
  17.2 15.8 %collective-permute-start.2 = (f32[528,128]{1,0:T(8,128)}, f32[528,128]{1,0:T(8,128)S(1)}, u32[]{:S(2)}, u32[]{:S(2)}) collective-permute-start(f32[528,128]{1,0:T(8,128)} %get-tuple-element.41), channel_id=1, source_target_pairs={{0,4},{4,8},{8,12},{12,16},{16,20},{20,24},{24,28},{28,0},{1,5},{5... | collective-permute-start | bytes 811016 | tf_op jit(solution)/shard_map/ppermute | solution.py:610
  17.4 56.6 %collective-permute-start.4 = (f32[1120,128]{1,0:T(8,128)S(1)}, f32[1120,128]{1,0:T(8,128)S(1)}, u32[]{:S(2)}, u32[]{:S(2)}) collective-permute-start(f32[1120,128]{1,0:T(8,128)S(1)} %copy-done.19), channel_id=1, source_target_pairs={{0,32},{32,64},{64,96},{96,128},{128,160},{160,192},{192,224},{224... | collective-permute-start | bytes 1720328 | tf_op jit(solution)/shard_map/ppermute | solution.py:610
  17.4 15.6 %collective-permute-start.3 = (f32[384,128]{1,0:T(8,128)}, f32[384,128]{1,0:T(8,128)S(1)}, u32[]{:S(2)}, u32[]{:S(2)}) collective-permute-start(f32[384,128]{1,0:T(8,128)} %get-tuple-element.42), channel_id=1, source_target_pairs={{0,28},{4,0},{8,4},{12,8},{16,12},{20,16},{24,20},{28,24},{1,29},{... | collective-permute-start | bytes 589832 | tf_op jit(solution)/shard_map/ppermute | solution.py:610
  33.0 0.7 copy-start.3
  33.7 0.7 copy-start.1
  36.8 37.2 %collective-permute-start.5 = (f32[632,128]{1,0:T(8,128)}, f32[632,128]{1,0:T(8,128)S(1)}, u32[]{:S(2)}, u32[]{:S(2)}) collective-permute-start(f32[632,128]{1,0:T(8,128)} %get-tuple-element.46), channel_id=1, source_target_pairs={{0,32},{32,64},{64,96},{96,128},{128,160},{160,192},{192,224},{224... | collective-permute-start | bytes 970760 | tf_op jit(solution)/shard_map/ppermute | solution.py:610
  42.4 31.6 %collective-permute-start.6 = (f32[408,128]{1,0:T(8,128)}, f32[408,128]{1,0:T(8,128)S(1)}, u32[]{:S(2)}, u32[]{:S(2)}) collective-permute-start(f32[408,128]{1,0:T(8,128)} %get-tuple-element.47), channel_id=1, source_target_pairs={{0,224},{32,0},{64,32},{96,64},{128,96},{160,128},{192,160},{224,1... | collective-permute-start | bytes 626696 | tf_op jit(solution)/shard_map/ppermute | solution.py:610
  74.0 0.7 copy-start.2
  74.0 0.9 copy-start.4
  74.9 0.7 copy-start
  85.7 3.9 %collective-permute-start.7 = (f32[16,128]{1,0:T(8,128)}, f32[16,128]{1,0:T(8,128)S(1)}, u32[]{:S(2)}, u32[]{:S(2)}) collective-permute-start(f32[16,128]{1,0:T(8,128)} %get-tuple-element.53), channel_id=1, source_target_pairs={{0,1},{1,2},{2,3},{3,0},{4,5},{5,6},{6,7},{7,4},{8,9},{9,10},{10,1... | collective-permute-start | bytes 24584 | tf_op jit(solution)/shard_map/ppermute | solution.py:610
  86.0 5.1 %collective-permute-start.8 = (f32[16,128]{1,0:T(8,128)}, f32[16,128]{1,0:T(8,128)S(1)}, u32[]{:S(2)}, u32[]{:S(2)}) collective-permute-start(f32[16,128]{1,0:T(8,128)} %get-tuple-element.54), channel_id=1, source_target_pairs={{0,3},{1,0},{2,1},{3,2},{4,7},{5,4},{6,5},{7,6},{8,11},{9,8},{10,9... | collective-permute-start | bytes 24584 | tf_op jit(solution)/shard_map/ppermute | solution.py:610
  89.6 1.5 copy-start.15
  93.3 6.2 %collective-permute-start.10 = (f32[80,128]{1,0:T(8,128)}, f32[80,128]{1,0:T(8,128)S(1)}, u32[]{:S(2)}, u32[]{:S(2)}) collective-permute-start(f32[80,128]{1,0:T(8,128)} %get-tuple-element.56), channel_id=1, source_target_pairs={{0,28},{4,0},{8,4},{12,8},{16,12},{20,16},{24,20},{28,24},{1,29},{... | collective-permute-start | bytes 122888 | tf_op jit(solution)/shard_map/ppermute | solution.py:610
  97.5 6.3 %collective-permute-start.9 = (f32[80,128]{1,0:T(8,128)}, f32[80,128]{1,0:T(8,128)S(1)}, u32[]{:S(2)}, u32[]{:S(2)}) collective-permute-start(f32[80,128]{1,0:T(8,128)} %get-tuple-element.55), channel_id=1, source_target_pairs={{0,4},{4,8},{8,12},{12,16},{16,20},{20,24},{24,28},{28,0},{1,5},{5... | collective-permute-start | bytes 122888 | tf_op jit(solution)/shard_map/ppermute | solution.py:610
  99.5 4.3 %copy-start.11 = (f32[80,128]{1,0:T(8,128)}, f32[80,128]{1,0:T(8,128)S(1)}, u32[]{:S(2)}) copy-start(f32[80,128]{1,0:T(8,128)S(1)} %collective-permute-done.10.y_high) | copy-start | bytes 122884
  106.3 14.8 %collective-permute-start.11 = (f32[264,128]{1,0:T(8,128)}, f32[264,128]{1,0:T(8,128)S(1)}, u32[]{:S(2)}, u32[]{:S(2)}) collective-permute-start(f32[264,128]{1,0:T(8,128)} %get-tuple-element.59), channel_id=1, source_target_pairs={{0,32},{32,64},{64,96},{96,128},{128,160},{160,192},{192,224},{224... | collective-permute-start | bytes 405512 | tf_op jit(solution)/shard_map/ppermute | solution.py:610
  106.3 14.8 %collective-permute-start.12 = (f32[264,128]{1,0:T(8,128)}, f32[264,128]{1,0:T(8,128)S(1)}, u32[]{:S(2)}, u32[]{:S(2)}) collective-permute-start(f32[264,128]{1,0:T(8,128)} %get-tuple-element.60), channel_id=1, source_target_pairs={{0,224},{32,0},{64,32},{96,64},{128,96},{160,128},{192,160},{224,1... | collective-permute-start | bytes 405512 | tf_op jit(solution)/shard_map/ppermute | solution.py:610
  121.0 0.7 copy-start.10
  126.5 3.9 %collective-permute-start.13 = (f32[16,128]{1,0:T(8,128)}, f32[16,128]{1,0:T(8,128)S(1)}, u32[]{:S(2)}, u32[]{:S(2)}) collective-permute-start(f32[16,128]{1,0:T(8,128)} %get-tuple-element.63), channel_id=1, source_target_pairs={{0,1},{1,2},{2,3},{3,0},{4,5},{5,6},{6,7},{7,4},{8,9},{9,10},{10,1... | collective-permute-start | bytes 24584 | tf_op jit(solution)/shard_map/ppermute | solution.py:610
  126.9 5.1 %collective-permute-start.14 = (f32[16,128]{1,0:T(8,128)}, f32[16,128]{1,0:T(8,128)S(1)}, u32[]{:S(2)}, u32[]{:S(2)}) collective-permute-start(f32[16,128]{1,0:T(8,128)} %get-tuple-element.64), channel_id=1, source_target_pairs={{0,3},{1,0},{2,1},{3,2},{4,7},{5,4},{6,5},{7,6},{8,11},{9,8},{10,9... | collective-permute-start | bytes 24584 | tf_op jit(solution)/shard_map/ppermute | solution.py:610
  130.3 1.7 %copy-start.16 = (f32[16,128]{1,0:T(8,128)}, f32[16,128]{1,0:T(8,128)S(1)}, u32[]{:S(2)}) copy-start(f32[16,128]{1,0:T(8,128)S(1)} %collective-permute-done.13.z_low) | copy-start | bytes 24580
  134.2 6.3 %collective-permute-start.15 = (f32[80,128]{1,0:T(8,128)}, f32[80,128]{1,0:T(8,128)S(1)}, u32[]{:S(2)}, u32[]{:S(2)}) collective-permute-start(f32[80,128]{1,0:T(8,128)} %get-tuple-element.65), channel_id=1, source_target_pairs={{0,4},{4,8},{8,12},{12,16},{16,20},{20,24},{24,28},{28,0},{1,5},{5... | collective-permute-start | bytes 122888 | tf_op jit(solution)/shard_map/ppermute | solution.py:610
  134.2 6.3 %collective-permute-start.16 = (f32[80,128]{1,0:T(8,128)}, f32[80,128]{1,0:T(8,128)S(1)}, u32[]{:S(2)}, u32[]{:S(2)}) collective-permute-start(f32[80,128]{1,0:T(8,128)} %get-tuple-element.66), channel_id=1, source_target_pairs={{0,28},{4,0},{8,4},{12,8},{16,12},{20,16},{24,20},{28,24},{1,29},{... | collective-permute-start | bytes 122888 | tf_op jit(solution)/shard_map/ppermute | solution.py:610
  143.6 14.8 %collective-permute-start.17 = (f32[264,128]{1,0:T(8,128)}, f32[264,128]{1,0:T(8,128)S(1)}, u32[]{:S(2)}, u32[]{:S(2)}) collective-permute-start(f32[264,128]{1,0:T(8,128)} %get-tuple-element.69), channel_id=1, source_target_pairs={{0,32},{32,64},{64,96},{96,128},{128,160},{160,192},{192,224},{224... | collective-permute-start | bytes 405512 | tf_op jit(solution)/shard_map/ppermute | solution.py:610
  143.6 14.8 %collective-permute-start.18 = (f32[264,128]{1,0:T(8,128)}, f32[264,128]{1,0:T(8,128)S(1)}, u32[]{:S(2)}, u32[]{:S(2)}) collective-permute-start(f32[264,128]{1,0:T(8,128)} %get-tuple-element.70), channel_id=1, source_target_pairs={{0,224},{32,0},{64,32},{96,64},{128,96},{160,128},{192,160},{224,1... | collective-permute-start | bytes 405512 | tf_op jit(solution)/shard_map/ppermute | solution.py:610
  158.4 0.7 copy-start.7
  158.4 0.7 copy-start.9
  (7 other events, 4.3 us)

commit v2 on v1

v2 whole, which is shorter than its diff:
```python
import functools
import math

import jax
import jax.numpy as jnp
from jax import lax
from jax.experimental import pallas as pl
from jax.experimental.pallas import tpu as pltpu
from jax.sharding import PartitionSpec as P

STEPS = 2
C_BOND = 3.0
DT_STEP = 0.04
REACH = 3
NEAR = 2
LANES = 128
SLOT = 16
PAD = 8
HALF_DT = 0.5 * DT_STEP


def half_offsets():
    result = []
    for step_x in range(0, 4):
        for step_y in range(-3, 4):
            for step_z in range(-3, 4):
                square = step_x * step_x + step_y * step_y + step_z * step_z
                if square == 0 or square > 9:
                    continue
                if step_x > 0 or (step_x == 0 and (step_y > 0 or (step_y == 0 and step_z > 0))):
                    result.append((step_x, step_y, step_z))
    return result


OFFSETS = half_offsets()
BONDS = {step: [] for step in range(-REACH, REACH + 1)}
for _plane, (_a, _b, _c) in enumerate(OFFSETS):
    BONDS[_a].append((_b, _c, _plane, True))
    BONDS[-_a].append((-_b, -_c, _plane, False))


def inner_layers(step, extent):
    return max(0, -step), min(extent, extent - step)


def outer_layers(step, extent):
    return (extent - step, extent) if step > 0 else (0, -step)


STEPS_ALL = list(range(-REACH, REACH + 1))
STEPS_OUT = [step for step in STEPS_ALL if step != 0]


def tiled_bonds(step, tiles):
    early, late = [], []
    for tile in range(tiles):
        for bond in BONDS[step]:
            low, high = 8 * tile + bond[0], 8 * tile + 8 + bond[0]
            (early if low >= 0 and high <= 8 * tiles else late).append((tile, *bond))
    return early, late


def inner_plan(extent, late):
    plan, total = [], 0
    for step in STEPS_ALL:
        bonds = tiled_bonds(step, extent[1] // 8)[int(late)]
        first, last = inner_layers(step, extent[0])
        plan.append((step, first, last, bonds, total))
        total += (last - first) * len(bonds)
    return plan, total


def outer_plan(extent):
    plan, total = [], 0
    for step in STEPS_OUT:
        bonds = [(tile, *bond) for tile in range(extent[1] // 8) for bond in BONDS[step]]
        first, last = outer_layers(step, extent[0])
        plan.append((step, first, last, bonds, total))
        total += (last - first) * len(bonds)
    return plan, total


def reach_z(distance):
    return max(abs(c) for a, b, c in OFFSETS if a >= distance)


def round_up(count):
    return (count + 7) // 8 * 8


def running(amounts):
    places, total = {}, 0
    for plane, amount in amounts:
        places[plane] = total
        total += amount
    return places, total


Z_UP, Z_UP_COUNT = running([(k, c) for k, (a, b, c) in enumerate(OFFSETS) if c > 0])
Z_DOWN, Z_DOWN_COUNT = running([(k, -c) for k, (a, b, c) in enumerate(OFFSETS) if c < 0])
Y_UP, Y_UP_COUNT = running([(k, b) for k, (a, b, c) in enumerate(OFFSETS) if b > 0])
Y_DOWN, Y_DOWN_COUNT = running([(k, -b) for k, (a, b, c) in enumerate(OFFSETS) if b < 0])
X_UP, X_UP_COUNT = running([(k, a) for k, (a, b, c) in enumerate(OFFSETS) if a > 0])
XY_UP, XY_UP_COUNT = running([(k, a * abs(b)) for k, (a, b, c) in enumerate(OFFSETS) if a * abs(b) > 0])


def lanes_like(value):
    return lax.broadcasted_iota(jnp.int32, value.shape, value.ndim - 1)


def rolled(value, shift):
    shift = shift % LANES
    return value if shift == 0 else pltpu.roll(value, shift, value.ndim - 1)


def beside_columns(low_pack, high_pack, lane_of):
    lanes = lanes_like(low_pack)
    return jnp.where(
        lanes < REACH, rolled(high_pack, -lane_of), rolled(low_pack, LANES - REACH - lane_of)
    )


def moved(main, beside, step):
    if step == 0:
        return main
    lanes = lanes_like(main)
    if step > 0:
        return rolled(jnp.where(lanes < step, beside, main), -step)
    return rolled(jnp.where(lanes >= LANES + step, beside, main), -step)


def pack_columns(field_of, count, extent, height):
    lanes = lax.broadcasted_iota(jnp.int32, (height, LANES), 1)
    up = jnp.zeros((height, LANES), jnp.float32)
    down = up
    for layer in range(extent):
        for field in range(count):
            lane_of = layer * SLOT + field * REACH
            value = field_of(field, layer)
            here = (lanes >= lane_of) & (lanes < lane_of + REACH)
            up = jnp.where(here, rolled(value, lane_of - (LANES - REACH)), up)
            down = jnp.where(here, rolled(value, lane_of), down)
    return up, down


def kept(flag, value):
    return jnp.where(flag > 0, value, 0.0)


def start_kernel(
    extent, pressure_in, motion_in, stiffness_in, borehole_in, flags_in, broken_in,
    motion, stiffness, pore, z_up, z_down, rows_up, rows_down, x_up,
    broken, pressure, borehole, flags, field_sems, layer_sems,
):
    size_x, size_y, _ = extent
    pairs = (
        (pressure_in, pressure), (borehole_in, borehole), (flags_in, flags),
        (motion_in, motion), (stiffness_in, stiffness),
    )
    copies = [
        pltpu.make_async_copy(source, target, field_sems.at[place])
        for place, (source, target) in enumerate(pairs)
    ]

    def layer_copy(layer):
        return pltpu.make_async_copy(
            broken_in.at[:, layer], broken.at[:, layer], layer_sems.at[layer]
        )

    for copy in copies:
        copy.start()
    for layer in range(size_x):
        layer_copy(layer).start()
    for copy in copies:
        copy.wait()
    ids = borehole[...]
    level = jnp.zeros(ids.shape, jnp.float32)
    for label in range(pressure.shape[0]):
        level = jnp.where(ids == label, pressure[label], level)
    pore[...] = flags[...].astype(jnp.float32) * level

    def field_of(field, layer):
        if field < 3:
            return motion[field, layer]
        return stiffness[layer] if field == 3 else pore[layer]

    up, down = pack_columns(field_of, 5, size_x, size_y)
    z_up[0:size_y] = up
    z_down[0:size_y] = down

    def one_layer(layer, carry):
        layer_copy(layer).wait()
        lanes = lax.broadcasted_iota(jnp.int32, (size_y, LANES), 1)
        rows = pl.ds(size_y + layer * size_y, size_y)
        up = jnp.zeros((size_y, LANES), jnp.float32)
        down = up
        for plane, (_, _, c) in enumerate(OFFSETS):
            if c > 0:
                at = Z_UP[plane]
                value = broken[plane, layer].astype(jnp.float32)
                up = jnp.where((lanes >= at) & (lanes < at + c), rolled(value, at + c), up)
            if c < 0:
                at = Z_DOWN[plane]
                value = broken[plane, layer].astype(jnp.float32)
                down = jnp.where((lanes >= at) & (lanes < at - c), rolled(value, at), down)
        z_up[rows] = up
        z_down[rows] = down
        return carry

    lax.fori_loop(0, size_x, one_layer, 0)
    for plane, (a, _, _) in enumerate(OFFSETS):
        for layer in range(a):
            at = (X_UP[plane] + layer) * size_y
            x_up[at : at + size_y] = broken[plane, size_x - a + layer].astype(jnp.float32)
    for plane, (_, b, _) in enumerate(OFFSETS):
        for layer in range(size_x):
            if b > 0:
                at = PAD + Y_UP[plane] * size_x + layer * b
                rows_up[at : at + b] = broken[plane, layer, size_y - b : size_y].astype(jnp.float32)
            if b < 0:
                at = PAD + Y_DOWN[plane] * size_x - layer * b
                rows_down[at : at - b] = broken[plane, layer, 0:-b].astype(jnp.float32)


def copy_y_rows(field_of, count, extent, low_pack, high_pack, y_up, y_down):
    size_x, size_y, _ = extent
    for field in range(count):
        for layer in range(size_x):
            at = (field * size_x + layer) * REACH
            y_up[at : at + REACH] = field_of(field, layer, slice(size_y - REACH, size_y))
            y_down[at : at + REACH] = field_of(field, layer, slice(0, REACH))
    at = count * size_x * REACH
    for pack in (low_pack, high_pack):
        y_up[at : at + REACH] = pack[size_y - REACH : size_y]
        y_down[at : at + REACH] = pack[0:REACH]
        at += REACH
    return at


def y_rows_kernel(extent, edges, motion, z_low, z_high, y_up, y_down):
    size_y = extent[1]
    low_pack = kept(edges[0], z_low[0:size_y])
    high_pack = kept(edges[1], z_high[0:size_y])
    copy_y_rows(
        lambda field, layer, rows: motion[field, layer, rows],
        3, extent, low_pack, high_pack, y_up, y_down,
    )


def y_rows_first_kernel(extent, edges, motion, stiffness, pore, z_low, z_high, y_up, y_down):
    size_x, size_y, _ = extent
    low_pack = kept(edges[0], z_low[0:size_y])
    high_pack = kept(edges[1], z_high[0:size_y])

    def field_of(field, layer, rows):
        if field < 3:
            return motion[field, layer, rows]
        return stiffness[layer, rows] if field == 3 else pore[layer, rows]

    base = copy_y_rows(field_of, 5, extent, low_pack, high_pack, y_up, y_down)
    for order, pack in enumerate((z_low, z_high)):
        for layer in range(size_x):
            first = size_y + layer * size_y
            at = base + (order * size_x + layer) * REACH
            y_up[at : at + REACH] = pack[first + size_y - REACH : first + size_y]
            y_down[at : at + REACH] = pack[first : first + REACH]


def widen(target, low_rows, middle, high_rows):
    size_y = middle.shape[0]
    target[0:REACH] = low_rows
    target[REACH : REACH + size_y] = middle
    target[REACH + size_y : 2 * REACH + size_y] = high_rows
    height = target.shape[0]
    target[2 * REACH + size_y : height] = jnp.zeros((height - 2 * REACH - size_y, LANES), jnp.float32)


def widen_fields(edges, field_of, count, extent, z_low, z_high, y_low, y_high, target, wide_pack):
    size_x, size_y, _ = extent
    for field in range(count):
        for layer in range(size_x):
            at = (field * size_x + layer) * REACH
            widen(
                target(field).at[layer],
                kept(edges[2], y_low[at : at + REACH]),
                field_of(field, layer),
                kept(edges[3], y_high[at : at + REACH]),
            )
    at = count * size_x * REACH
    for order, pack in enumerate((z_low, z_high)):
        widen(
            wide_pack.at[order],
            kept(edges[2], y_low[at : at + REACH]),
            kept(edges[order], pack[0:size_y]),
            kept(edges[3], y_high[at : at + REACH]),
        )
        at += REACH
    return at


def copy_x_layers(count, size_x, target, wide_pack, x_up, x_down):
    height = wide_pack.shape[1]
    for field in range(count):
        for layer in range(REACH):
            at = (field * REACH + layer) * height
            x_up[at : at + height] = target(field)[size_x - REACH + layer]
            x_down[at : at + height] = target(field)[layer]
    at = count * REACH * height
    for order in range(2):
        x_up[at : at + height] = wide_pack[order]
        x_down[at : at + height] = wide_pack[order]
        at += height
    return at


def x_layers_kernel(
    extent, edges, motion, z_low, z_high, y_low, y_high, x_up, x_down, wide, wide_pack
):
    widen_fields(
        edges, lambda field, layer: motion[field, layer],
        3, extent, z_low, z_high, y_low, y_high, lambda field: wide.at[field], wide_pack,
    )
    copy_x_layers(3, extent[0], lambda field: wide.at[field], wide_pack, x_up, x_down)


def x_layers_first_kernel(
    extent, edges, motion, stiffness, pore, z_low, z_high, y_low, y_high, rows_low, rows_high,
    wide_static, wide_pack, wide_broken, x_up, x_down, wide,
):
    size_x, size_y, _ = extent

    def field_of(field, layer):
        if field < 3:
            return motion[field, layer]
        return stiffness[layer] if field == 3 else pore[layer]

    def target(field):
        return wide.at[field] if field < 3 else wide_static.at[field - 3]

    base = widen_fields(
        edges, field_of, 5, extent, z_low, z_high, y_low, y_high, target, wide_pack
    )
    for order, pack in enumerate((z_low, z_high)):
        for layer in range(size_x):
            first = size_y + layer * size_y
            at = base + (order * size_x + layer) * REACH
            widen(
                wide_broken.at[order, layer],
                y_low[at : at + REACH],
                pack[first : first + size_y],
                y_high[at : at + REACH],
            )
    at = copy_x_layers(4, size_x, target, wide_pack, x_up, x_down)
    height = wide.shape[2]
    x_up[at : at + height] = wide_static[1, size_x - 1]
    x_down[at : at + height] = wide_static[1, 0]
    at += height
    for order in range(2):
        for layer in range(NEAR):
            x_up[at : at + height] = wide_broken[order, size_x - NEAR + layer]
            at += height
    for plane, (a, b, _) in enumerate(OFFSETS):
        if a * b == 0:
            continue
        rows, many = abs(b), a * abs(b)
        source = rows_low if b > 0 else rows_high
        first = PAD + (Y_UP if b > 0 else Y_DOWN)[plane] * size_x + (size_x - a) * rows
        x_up[at + XY_UP[plane] : at + XY_UP[plane] + many] = source[first : first + many]


def each_shift(main, low_pack, high_pack, lane_of, add_step, reach=REACH):
    beside = beside_columns(low_pack, high_pack, lane_of) if reach else None
    for step in range(-reach, reach + 1):
        value = moved(main, beside, step)
        yield step + REACH, value + float(step) if add_step and step else value


def wanted_keep(value, low, high, plane, step_z):
    if step_z == 0:
        return 1.0 - value
    lanes = lanes_like(value)
    if step_z < 0:
        beside = rolled(low(), -Z_UP[plane])
        value = jnp.where(lanes < -step_z, beside, rolled(value, -step_z))
    else:
        beside = rolled(high(), LANES - step_z - Z_DOWN[plane])
        value = jnp.where(lanes >= LANES - step_z, beside, rolled(value, -step_z))
    return 1.0 - value


def weights_early_kernel(
    extent, edges, broken_in, stiffness, z_low, z_high, weights, keeps, shifts, planes, broken, sems
):
    size_x, size_y, _ = extent

    def layer_copy(layer):
        return pltpu.make_async_copy(broken_in.at[:, layer], broken.at[:, layer], sems.at[layer])

    for layer in range(size_x):
        layer_copy(layer).start()
    low_pack = kept(edges[0], z_low[0:size_y])
    high_pack = kept(edges[1], z_high[0:size_y])
    for layer in range(size_x):
        for order, value in each_shift(
            stiffness[layer], low_pack, high_pack, layer * SLOT + 3 * REACH, False
        ):
            shifts[order, layer, REACH : REACH + size_y] = value

    def fill(layer, carry):
        layer_copy(layer).wait()
        for plane in range(len(OFFSETS)):
            planes[plane, layer, REACH : REACH + size_y] = broken[plane, layer].astype(jnp.float32)
        return carry

    lax.fori_loop(0, size_x, fill, 0)
    for late, target in ((False, weights), (True, keeps)):
        for step, first, last, bonds, base in inner_plan(extent, late)[0]:

            def one_layer(layer, carry, step=step, first=first, bonds=bonds, base=base):
                slot = base + (layer - first) * len(bonds)
                far_layer = layer + step
                for order, (tile, step_y, step_z, plane, owner) in enumerate(bonds):
                    rows = slice(8 * tile, 8 * tile + 8)
                    far_rows = slice(REACH + step_y + 8 * tile, REACH + step_y + 8 * tile + 8)
                    if owner:
                        keep = 1.0 - broken[plane, layer, rows].astype(jnp.float32)
                    else:
                        at = size_y + far_layer * size_y + step_y + 8 * tile
                        keep = wanted_keep(
                            planes[plane, far_layer, far_rows],
                            lambda: z_low[pl.ds(at, 8)],
                            lambda: z_high[pl.ds(at, 8)],
                            plane, step_z,
                        )
                    keep = (0.5 * C_BOND) * keep
                    if not late:
                        far = shifts[step_z + REACH, far_layer, far_rows]
                        keep = jnp.where(far > 0.0, keep * (stiffness[layer, rows] + far), 0.0)
                    target[slot + order] = keep
                return carry

            lax.fori_loop(first, last, one_layer, 0)


def weights_late_kernel(
    extent, stiffness, wide, wide_pack, wide_broken, rows_low, rows_high, keeps, weights, shifts
):
    size_x, size_y, _ = extent
    for layer in range(size_x):
        for order, value in each_shift(
            wide[0, layer], wide_pack[0], wide_pack[1], layer * SLOT + 3 * REACH, False
        ):
            shifts[order, layer] = value
    for step, first, last, bonds, base in inner_plan(extent, True)[0]:

        def one_layer(layer, carry, step=step, first=first, bonds=bonds, base=base):
            slot = base + (layer - first) * len(bonds)
            far_layer = layer + step
            sublanes = lax.broadcasted_iota(jnp.int32, (8, LANES), 0)
            for order, (tile, step_y, step_z, plane, owner) in enumerate(bonds):
                rows = slice(8 * tile, 8 * tile + 8)
                far_rows = slice(REACH + step_y + 8 * tile, REACH + step_y + 8 * tile + 8)
                keep = keeps[slot + order]
                if not owner:
                    if step_y < 0:
                        at = PAD + Y_UP[plane] * size_x - far_layer * step_y
                        value = rows_low[pl.ds(at, 8)]
                        across = sublanes < -step_y
                    else:
                        at = PAD + Y_DOWN[plane] * size_x + far_layer * step_y + step_y - 8
                        value = rows_high[pl.ds(at, 8)]
                        across = sublanes >= 8 - step_y
                    halo = wanted_keep(
                        value,
                        lambda: wide_broken[0, far_layer, far_rows],
                        lambda: wide_broken[1, far_layer, far_rows],
                        plane, step_z,
                    )
                    keep = jnp.where(across, (0.5 * C_BOND) * halo, keep)
                far = shifts[step_z + REACH, far_layer, far_rows]
                weights[slot + order] = jnp.where(
                    far > 0.0, keep * (stiffness[layer, rows] + far), 0.0
                )
            return carry

        lax.fori_loop(first, last, one_layer, 0)


def weights_outer_kernel(
    extent, edges, stiffness, pore, wide, wide_pack, x_up, x_broken, x_low, x_high,
    weights, pressing, shifts, planes,
):
    size_x, size_y, _ = extent
    height = wide.shape[2]
    pack_at = 4 * REACH * height
    pore_at = pack_at + 2 * height
    broken_at = pore_at + height
    rows_at = broken_at + 2 * NEAR * height

    def pack_of(source, order):
        return source[pack_at + order * height : pack_at + (order + 1) * height]

    for side, source in enumerate((x_low, x_high)):
        packs = [kept(edges[4 + side], pack_of(source, order)) for order in range(2)]
        for layer in range(REACH):
            at = (3 * REACH + layer) * height
            from_layer = size_x - REACH + layer if side == 0 else layer
            distance = REACH - layer if side == 0 else layer + 1
            for order, value in each_shift(
                kept(edges[4 + side], source[at : at + height]), *packs,
                from_layer * SLOT + 3 * REACH, False, reach_z(distance),
            ):
                shifts[order, side * REACH + layer] = value
    for plane, (a, b, _) in enumerate(OFFSETS):
        for layer in range(a):
            at = (X_UP[plane] + layer) * size_y
            place = X_UP[plane] + layer
            planes[place, REACH : REACH + size_y] = x_broken[at : at + size_y]
            at = rows_at + XY_UP.get(plane, 0) + layer * abs(b)
            if b > 0:
                planes[place, REACH - b : REACH] = x_low[at : at + b]
            if b < 0:
                planes[place, REACH + size_y : REACH + size_y - b] = x_low[at : at - b]
    for step, first, last, bonds, base in outer_plan(extent)[0]:
        for layer in range(first, last):
            slot = base + (layer - first) * len(bonds)
            far_layer = layer + step
            far_layer = far_layer + REACH if far_layer < 0 else far_layer - size_x + REACH
            for order, (tile, step_y, step_z, plane, owner) in enumerate(bonds):
                rows = slice(8 * tile, 8 * tile + 8)
                far_rows = slice(REACH + step_y + 8 * tile, REACH + step_y + 8 * tile + 8)
                far = shifts[step_z + REACH, far_layer, far_rows]
                if owner:
                    at = (X_UP[plane] + layer - first) * size_y + 8 * tile
                    keep = 1.0 - x_up[at : at + 8]
                else:
                    low_at = broken_at + (far_layer + NEAR - REACH) * height
                    high_at = low_at + NEAR * height
                    keep = wanted_keep(
                        planes[X_UP[plane] + layer, far_rows],
                        lambda: x_low[far_rows.start + low_at : far_rows.stop + low_at],
                        lambda: x_low[far_rows.start + high_at : far_rows.stop + high_at],
                        plane, step_z,
                    )
                value = keep * (0.5 * C_BOND) * (stiffness[layer, rows] + far)
                weights[slot + order] = jnp.where(far > 0.0, value, 0.0)

    middle = slice(REACH, REACH + size_y)

    def wide_field(field, layer):
        if layer < 0 or layer >= size_x:
            source = x_low if layer < 0 else x_high
            at = (field * REACH + (layer + REACH if layer < 0 else layer - size_x)) * height
            at = pore_at if field == 4 else at
            return kept(edges[4 if layer < 0 else 5], source[at : at + height])
        return wide[field - 3, layer]

    for layer in range(size_x):
        own = pore[layer]
        for axis in range(3):
            total = jnp.zeros((size_y, LANES), jnp.float32)
            for sign in (1, -1):
                if axis == 0:
                    inside = wide_field(3, layer + sign)[middle]
                    level = wide_field(4, layer + sign)[middle]
                elif axis == 1:
                    rows = slice(REACH + sign, REACH + sign + size_y)
                    inside = wide[0, layer, rows]
                    level = wide[1, layer, rows]
                else:
                    inside, level = (
                        moved(
                            wide[field - 3, layer],
                            beside_columns(
                                wide_pack[0], wide_pack[1], layer * SLOT + field * REACH
                            ),
                            sign,
                        )[middle]
                        for field in (3, 4)
                    )
                total = total + jnp.where(inside > 0.0, (-0.5 * sign) * (level - own), 0.0)
            pressing[axis, layer] = total


def add_bonds(bonds, step, layer, far_layer, motion, shifts, weights, slot, total):
    for tile in sorted({bond[0] for bond in bonds}):
        rows = slice(8 * tile, 8 * tile + 8)
        own = [motion[axis, layer, rows] for axis in range(3)]
        near_x = own[0] - float(step)
        near_y = {step_y: own[1] - float(step_y) for step_y in range(-REACH, REACH + 1)}
        force = [total[axis, layer, rows] for axis in range(3)]
        for order, (bond_tile, step_y, step_z, plane, _) in enumerate(bonds):
            if bond_tile != tile:
                continue
            far_rows = slice(REACH + step_y + 8 * tile, REACH + step_y + 8 * tile + 8)
            far = [shifts[step_z + REACH, axis, far_layer, far_rows] for axis in range(3)]
            radial = [far[0] - near_x, far[1] - near_y[step_y], far[2] - own[2]]
            square = radial[0] * radial[0] + radial[1] * radial[1] + radial[2] * radial[2]
            rest = math.sqrt(sum(part * part for part in OFFSETS[plane]))
            factor = weights[slot + order] * (1.0 / rest - lax.rsqrt(square))
            force = [force[axis] + factor * radial[axis] for axis in range(3)]
        for axis in range(3):
            total[axis, layer, rows] = force[axis]


def add_inner(extent, late, motion, shifts, weights, total):
    for step, first, last, bonds, base in inner_plan(extent, late)[0]:
        if not bonds:
            continue

        def one_layer(layer, carry, step=step, first=first, bonds=bonds, base=base):
            slot = base + (layer - first) * len(bonds)
            add_bonds(bonds, step, layer, layer + step, motion, shifts, weights, slot, total)
            return carry

        lax.fori_loop(first, last, one_layer, 0)


def force_early_kernel(extent, edges, motion, z_low, z_high, weights, total, shifts):
    size_x, size_y, _ = extent
    total[...] = jnp.zeros(total.shape, jnp.float32)
    low_pack = kept(edges[0], z_low[0:size_y])
    high_pack = kept(edges[1], z_high[0:size_y])
    for layer in range(size_x):
        for axis in range(3):
            for order, value in each_shift(
                motion[axis, layer], low_pack, high_pack, layer * SLOT + axis * REACH, axis == 2
            ):
                shifts[order, axis, layer, REACH : REACH + size_y] = value
    add_inner(extent, False, motion, shifts, weights, total)


def force_late_kernel(
    extent, count, edges, motion, early, early_shifts, y_low, y_high, weights, total, shifts, halo
):
    size_x, size_y, _ = extent
    total[...] = early[...]
    shifts[...] = early_shifts[...]
    pack_at = count * size_x * REACH
    for order in range(2):
        at = pack_at + order * REACH
        halo[order, 0:REACH] = kept(edges[2], y_low[at : at + REACH])
        halo[order, REACH : 2 * REACH] = kept(edges[3], y_high[at : at + REACH])
        halo[order, 2 * REACH : 8] = jnp.zeros((8 - 2 * REACH, LANES), jnp.float32)
    low_pack, high_pack = halo[0], halo[1]
    for axis in range(3):
        for layer in range(size_x):
            at = (axis * size_x + layer) * REACH
            place = 2 + axis * size_x + layer
            halo[place, 0:REACH] = kept(edges[2], y_low[at : at + REACH])
            halo[place, REACH : 2 * REACH] = kept(edges[3], y_high[at : at + REACH])
            halo[place, 2 * REACH : 8] = jnp.zeros((8 - 2 * REACH, LANES), jnp.float32)
            for order, value in each_shift(
                halo[place], low_pack, high_pack, layer * SLOT + axis * REACH, axis == 2
            ):
                shifts[order, axis, layer, 0:REACH] = value[0:REACH]
                shifts[order, axis, layer, REACH + size_y : 2 * REACH + size_y] = value[
                    REACH : 2 * REACH
                ]
    add_inner(extent, True, motion, shifts, weights, total)


def finish_kernel(
    extent, count, height, stage, edges, motion, speed, pressing, inner, weights, x_low, x_high, *refs
):
    size_x, size_y, _ = extent
    if stage == "last":
        motion_out, speed_out, accel_out, total, shifts = refs
    else:
        motion_out, speed_out, z_up, z_down, total, shifts = refs
    total[...] = inner[...] + pressing[...]
    pack_at = count * REACH * height
    for side, source in enumerate((x_low, x_high)):
        packs = [
            kept(edges[4 + side], source[pack_at + order * height : pack_at + (order + 1) * height])
            for order in range(2)
        ]
        for layer in range(REACH):
            from_layer = size_x - REACH + layer if side == 0 else layer
            distance = REACH - layer if side == 0 else layer + 1
            for axis in range(3):
                at = (axis * REACH + layer) * height
                for order, value in each_shift(
                    kept(edges[4 + side], source[at : at + height]), *packs,
                    from_layer * SLOT + axis * REACH, axis == 2, reach_z(distance),
                ):
                    shifts[order, axis, side * REACH + layer] = value
    for step, first, last, bonds, base in outer_plan(extent)[0]:

        def one_layer(layer, carry, step=step, first=first, bonds=bonds, base=base):
            slot = base + (layer - first) * len(bonds)
            far_layer = layer + step + (REACH if step < 0 else REACH - size_x)
            add_bonds(bonds, step, layer, far_layer, motion, shifts, weights, slot, total)
            return carry

        lax.fori_loop(first, last, one_layer, 0)
    accel = total[...]
    new_speed = speed[...] + HALF_DT * accel
    if stage == "last":
        motion_out[...] = motion[...]
        speed_out[...] = new_speed
        accel_out[...] = accel
        return
    if stage == "middle":
        new_speed = new_speed + HALF_DT * accel
    speed_out[...] = new_speed
    motion_out[...] = motion[...] + DT_STEP * new_speed
    up, down = pack_columns(lambda axis, layer: motion_out[axis, layer], 3, size_x, size_y)
    z_up[...] = up
    z_down[...] = down


VMEM = pl.BlockSpec(memory_space=pltpu.VMEM)
SMEM = pl.BlockSpec(memory_space=pltpu.SMEM)


def call(kernel, scalars, operands, shapes, scratch=(), name=None, results=(), far=()):
    operands = [pltpu.with_memory_space_constraint(operand, pltpu.HBM) for operand in far] + [
        pltpu.with_memory_space_constraint(operand, pltpu.VMEM) for operand in operands
    ]
    return pl.pallas_call(
        kernel,
        out_shape=[
            jax.ShapeDtypeStruct(shape, jnp.float32)
            if place in results
            else pltpu.VMEM(shape, jnp.float32)
            for place, shape in enumerate(shapes)
        ],
        in_specs=[SMEM] * len(scalars)
        + [pl.BlockSpec(memory_space=pltpu.HBM)] * len(far)
        + [VMEM] * (len(operands) - len(far)),
        out_specs=[VMEM] * len(shapes),
        scratch_shapes=[
            pltpu.VMEM(item, jnp.float32) if isinstance(item, tuple) else item for item in scratch
        ],
        compiler_params=pltpu.CompilerParams(vmem_limit_bytes=24 * 1024 * 1024),
        name=name,
    )(*scalars, *operands)


def sent(value, axis, distance):
    count = lax.axis_size(axis)
    return lax.ppermute(value, axis, [(i, (i + distance) % count) for i in range(count)])


def on_device(displacement, velocity, stiffness, broken, borehole_id, flags, pressure):
    extent = stiffness.shape
    size_x, size_y, _ = extent
    height = size_y + 8
    edges = jnp.stack(
        [
            end
            for axis in ("gz", "gy", "gx")
            for end in (
                (lax.axis_index(axis) > 0).astype(jnp.int32),
                (lax.axis_index(axis) < lax.axis_size(axis) - 1).astype(jnp.int32),
            )
        ]
    )
    field = (size_x, size_y, LANES)
    vector = (3,) + field
    part = functools.partial

    pack = (size_y + size_x * size_y + PAD, LANES)
    rows_shapes = [(count * size_x + 2 * PAD, LANES) for count in (Y_UP_COUNT, Y_DOWN_COUNT)]
    layers_shape = (X_UP_COUNT * size_y, LANES)
    motion, stiffness, pore, z_up, z_down, rows_up, rows_down, x_up = pl.pallas_call(
        part(start_kernel, extent),
        out_shape=[
            pltpu.VMEM(shape, kind)
            for shape, kind in (
                (vector, jnp.float32), (field, jnp.float32),
                (field, jnp.float32), (pack, jnp.float32), (pack, jnp.float32),
                (rows_shapes[0], jnp.float32), (rows_shapes[1], jnp.float32),
                (layers_shape, jnp.float32),
            )
        ],
        in_specs=[pl.BlockSpec(memory_space=pltpu.HBM)] * 6,
        out_specs=[VMEM] * 8,
        scratch_shapes=[
            pltpu.VMEM(broken.shape, jnp.int32),
            pltpu.SMEM(pressure.shape, jnp.float32),
            pltpu.VMEM(field, jnp.int32),
            pltpu.VMEM(field, jnp.int32),
            pltpu.SemaphoreType.DMA((5,)),
            pltpu.SemaphoreType.DMA((size_x,)),
        ],
        compiler_params=pltpu.CompilerParams(vmem_limit_bytes=24 * 1024 * 1024),
        name="start",
    )(
        *(
            pltpu.with_memory_space_constraint(operand, pltpu.HBM)
            for operand in (pressure, displacement, stiffness, borehole_id, flags, broken)
        )
    )
    z_low = sent(z_up, "gz", 1)
    z_high = sent(z_down, "gz", -1)
    rows_low = sent(rows_up, "gy", 1)
    rows_high = sent(rows_down, "gy", -1)
    x_broken = sent(x_up, "gx", 1)
    rows = (round_up(5 * size_x * REACH + 2 * REACH + 2 * size_x * REACH), LANES)
    y_up, y_down = call(
        part(y_rows_first_kernel, extent), [edges],
        [motion, stiffness, pore, z_low, z_high], [rows, rows], name="y_rows_first",
    )
    y_low = sent(y_up, "gy", 1)
    y_high = sent(y_down, "gy", -1)
    moves = 2 * REACH + 1
    early_slots = inner_plan(extent, False)[1]
    late_slots = inner_plan(extent, True)[1]
    outer_slots = outer_plan(extent)[1]
    weights_early, keeps = call(
        part(weights_early_kernel, extent), [edges], [stiffness, z_low, z_high],
        [(early_slots, 8, LANES), (late_slots, 8, LANES)],
        [
            (moves, size_x, height, LANES),
            (len(OFFSETS), size_x, height, LANES),
            pltpu.VMEM(broken.shape, jnp.int32),
            pltpu.SemaphoreType.DMA((size_x,)),
        ], name="weights_early", far=[broken],
    )

    def force_early(motion, z_low, z_high):
        return call(
            part(force_early_kernel, extent), [edges], [motion, z_low, z_high, weights_early],
            [vector, (moves, 3, size_x, height, LANES)], name="force_early",
        )

    def force_late(count, motion, early, early_shifts, y_low, y_high):
        return call(
            part(force_late_kernel, extent, count), [edges],
            [motion, early, early_shifts, y_low, y_high, weights_late], [vector],
            [(moves, 3, size_x, height, LANES), (2 + 3 * size_x, 8, LANES)], name="force_late",
        )[0]

    early, early_shifts = force_early(motion, z_low, z_high)
    y_low, y_high, x_broken, early = lax.optimization_barrier((y_low, y_high, x_broken, early))
    layers = (4 * REACH + 3) * height
    wide_static, wide_pack, wide_broken, x_fields_up, x_fields_down = call(
        part(x_layers_first_kernel, extent), [edges],
        [motion, stiffness, pore, z_low, z_high, y_low, y_high, rows_low, rows_high],
        [
            (2, size_x, height, LANES),
            (2, height, LANES),
            (2, size_x, height, LANES),
            (round_up(layers + 2 * NEAR * height + XY_UP_COUNT), LANES),
            (layers, LANES),
        ], [(3, size_x, height, LANES)], name="x_layers_first",
    )
    x_low = sent(x_fields_up, "gx", 1)
    x_high = sent(x_fields_down, "gx", -1)
    (weights_late,) = call(
        part(weights_late_kernel, extent), [],
        [stiffness, wide_static, wide_pack, wide_broken, rows_low, rows_high, keeps],
        [(late_slots, 8, LANES)], [(moves, size_x, height, LANES)], name="weights_late",
    )
    inner = force_late(5, motion, early, early_shifts, y_low, y_high)
    outer_weights, pressing = call(
        part(weights_outer_kernel, extent), [edges],
        [stiffness, pore, wide_static, wide_pack, x_up, x_broken, x_low, x_high],
        [(outer_slots, 8, LANES), vector],
        [(moves, 2 * REACH, height, LANES), (X_UP_COUNT, height, LANES)],
        name="weights_outer",
    )

    def finish(stage, count, motion, speed, inner, x_low, x_high):
        columns = (size_y, LANES)
        shapes = [vector] * 3 if stage == "last" else [vector, vector, columns, columns]
        return call(
            part(finish_kernel, extent, count, height, stage), [edges],
            [motion, speed, pressing, inner, outer_weights, x_low, x_high],
            shapes, [vector, (moves, 3, 2 * REACH, height, LANES)], name="finish_" + stage,
            results=(0, 1, 2) if stage == "last" else (),
        )

    motion, speed, z_up, z_down = finish(
        "first", 4, motion, velocity, inner, x_low, x_high
    )
    for step_index in range(STEPS):
        z_low = sent(z_up, "gz", 1)
        z_high = sent(z_down, "gz", -1)
        rows = (round_up(3 * size_x * REACH + 2 * REACH), LANES)
        y_up, y_down = call(
            part(y_rows_kernel, extent), [edges], [motion, z_low, z_high], [rows, rows],
            name="y_rows",
        )
        y_low = sent(y_up, "gy", 1)
        y_high = sent(y_down, "gy", -1)
        early, early_shifts = force_early(motion, z_low, z_high)
        y_low, y_high, early = lax.optimization_barrier((y_low, y_high, early))
        layers = (3 * REACH + 2) * height
        x_up, x_down = call(
            part(x_layers_kernel, extent), [edges],
            [motion, z_low, z_high, y_low, y_high],
            [(layers, LANES), (layers, LANES)],
            [(3, size_x, height, LANES), (2, height, LANES)], name="x_layers",
        )
        x_low = sent(x_up, "gx", 1)
        x_high = sent(x_down, "gx", -1)
        inner = force_late(3, motion, early, early_shifts, y_low, y_high)
        if step_index < STEPS - 1:
            motion, speed, z_up, z_down = finish("middle", 3, motion, speed, inner, x_low, x_high)
        else:
            motion, speed, accel = finish("last", 3, motion, speed, inner, x_low, x_high)
    return (motion, speed, accel)


def solution(mesh):
    in_specs = (
        P(None, "gx", "gy", "gz"),
        P(None, "gx", "gy", "gz"),
        P("gx", "gy", "gz"),
        P(None, "gx", "gy", "gz"),
        P("gx", "gy", "gz"),
        P("gx", "gy", "gz"),
        P(),
    )
    out_specs = (P(None, "gx", "gy", "gz"), P(None, "gx", "gy", "gz"), P(None, "gx", "gy", "gz"))
    return jax.shard_map(
        on_device, mesh=mesh, in_specs=in_specs, out_specs=out_specs, check_vma=False
    )
```

time: 164 us -> 102 us (0.62)
  the two profiles are of different devices: /device:TPU:6 before, /device:TPU:71 now
where the time goes in v2:
time: 102 us
  Pallas kernels  52.9 us (52%)
  starting transfers between devices  32.1 us (31%)
  waiting for transfers between devices  15.9 us (16%)
    pallas_call x18, Pallas kernels, call(): pl.pallas_call(kernel, out_shape=[jax.ShapeDtypeStruct(shape, jnp.float32...  49 us
    ppermute x21, starting transfers between devices, sent(): lax.ppermute(value, axis, [(i, (i + distance) % count) for i in range(cou...  32.1 us
    ppermute x21, waiting for transfers between devices, sent(): lax.ppermute(value, axis, [(i, (i + distance) % count) for i in range(cou...  15.9 us
    pallas_call x1, Pallas kernels, on_device(): pl.pallas_call(part(start_kernel, extent), out_shape=[pltpu.VMEM(shape, k...  3.86 us
  transfers between devices with their start and end apart: 21, of which 8 were waited for; matrix products, arithmetic and copies ran while one was open for 0% of the time, Pallas kernels for 36%

profile of v2, /device:TPU:71, one launch (start us, length us, event | category | flops | bytes accessed | tf_op | source)
XLA Modules:
  0.0 101.8 jit_solution(8252211070982106451)
XLA Ops:
  0.6 3.9 %start.1 = (f32[3,8,16,128]{3,2,1,0:T(8,128)S(1)}, f32[8,16,128]{2,1,0:T(8,128)S(1)}, f32[8,16,128]{2,1,0:T(8,128)S(1)}, f32[152,128]{1,0:T(8,128)S(1)}, f32[152...) custom-call(f32[8]{0:T(128)} %pressure_in.1, ...), custom_call_target="tpu_custom_call" | custom-call | tf_op jit(solution)/shard_map/start/pallas_call | solution.py:767
  4.5 4.8 %collective-permute-start.4 = (f32[1120,128]{1,0:T(8,128)S(1)}, f32[1120,128]{1,0:T(8,128)S(1)}, u32[]{:S(2)}, u32[]{:S(2)}) collective-permute-start(f32[1120,128]{1,0:T(8,128)S(1)} %get-tuple-element.61.x_up), channel_id=1, source_target_pairs={{0,32},{32,64},{64,96},{96,128},{128,160},{160,192},{192,224},{224... | collective-permute-start | bytes 1720328 | tf_op jit(solution)/shard_map/ppermute | solution.py:743
  10.3 1.3 %collective-permute-start.1 = (f32[152,128]{1,0:T(8,128)S(1)}, f32[152,128]{1,0:T(8,128)S(1)}, u32[]{:S(2)}, u32[]{:S(2)}) collective-permute-start(f32[152,128]{1,0:T(8,128)S(1)} %get-tuple-element.58), channel_id=1, source_target_pairs={{0,3},{1,0},{2,1},{3,2},{4,7},{5,4},{6,5},{7,6},{8,11},{9,8},{10,9... | collective-permute-start | bytes 233480 | tf_op jit(solution)/shard_map/ppermute | solution.py:743
  11.5 2.8 %collective-permute-start.6 = (f32[224,128]{1,0:T(8,128)S(1)}, f32[224,128]{1,0:T(8,128)S(1)}, u32[]{:S(2)}, u32[]{:S(2)}) collective-permute-start(f32[224,128]{1,0:T(8,128)S(1)} %get-tuple-element.67), channel_id=1, source_target_pairs={{0,28},{4,0},{8,4},{12,8},{16,12},{20,16},{24,20},{28,24},{1,29},{... | collective-permute-start | bytes 344072 | tf_op jit(solution)/shard_map/ppermute | solution.py:743
  15.5 1.8 %collective-permute-start.2 = (f32[176,128]{1,0:T(8,128)S(1)}, f32[176,128]{1,0:T(8,128)S(1)}, u32[]{:S(2)}, u32[]{:S(2)}) collective-permute-start(f32[176,128]{1,0:T(8,128)S(1)} %get-tuple-element.59), channel_id=1, source_target_pairs={{0,4},{4,8},{8,12},{12,16},{16,20},{20,24},{24,28},{28,0},{1,5},{5... | collective-permute-start | bytes 270344 | tf_op jit(solution)/shard_map/ppermute | solution.py:743
  17.3 1.8 %collective-permute-start.3 = (f32[176,128]{1,0:T(8,128)S(1)}, f32[176,128]{1,0:T(8,128)S(1)}, u32[]{:S(2)}, u32[]{:S(2)}) collective-permute-start(f32[176,128]{1,0:T(8,128)S(1)} %get-tuple-element.60), channel_id=1, source_target_pairs={{0,28},{4,0},{8,4},{12,8},{16,12},{20,16},{24,20},{28,24},{1,29},{... | collective-permute-start | bytes 270344 | tf_op jit(solution)/shard_map/ppermute | solution.py:743
  19.1 8.0 %weights_early.1 = (f32[1024,8,128]{2,1,0:T(8,128)S(1)}, f32[648,8,128]{2,1,0:T(8,128)S(1)}) custom-call(s32[6]{0:T(128)S(1)} %stack.36.edges, s32[61,8,16,128]{3,2,1,0:T(8,128)} %broken_in.3, f32[8,16,128]{2,1,0:T(8,128)S(1)} %get-tuple-element.55.stiffness, f32[152,128]{1,0:T(8,128)S(1)} %collective-permute-done.z_low, ...), custom_call_target="tpu_custom_call" | custom-call | tf_op jit(solution)/shard_map/weights_early/pallas_call | solution.py:721
  27.1 5.2 %force_early.3 = (f32[3,8,16,128]{3,2,1,0:T(8,128)S(1)}, f32[7,3,8,24,128]{4,3,2,1,0:T(8,128)S(1)}) custom-call(s32[6]{0:T(128)S(1)} %stack.36.edges, f32[3,8,16,128]{3,2,1,0:T(8,128)S(1)} %get-tuple-element.54.motion, f32[152,128]{1,0:T(8,128)S(1)} %collective-permute-done.z_low, f32[152,128]{1,0:T(8,128)S(1)} %collective-permute-done.1.z_high, ...), custom_call_target="tpu_custom_call" | custom-call | tf_op jit(solution)/shard_map/force_early/pallas_call | solution.py:721
  33.1 3.1 %collective-permute-start.7 = (f32[536,128]{1,0:T(8,128)S(1)}, f32[536,128]{1,0:T(8,128)S(1)}, u32[]{:S(2)}, u32[]{:S(2)}) collective-permute-start(f32[536,128]{1,0:T(8,128)S(1)} %get-tuple-element.71), channel_id=1, source_target_pairs={{0,32},{32,64},{64,96},{96,128},{128,160},{160,192},{192,224},{224... | collective-permute-start | bytes 823304 | tf_op jit(solution)/shard_map/ppermute | solution.py:743
  36.2 2.9 %weights_late.1.weights = f32[648,8,128]{2,1,0:T(8,128)S(1)} custom-call(f32[8,16,128]{2,1,0:T(8,128)S(1)} %get-tuple-element.55.stiffness, f32[2,8,24,128]{3,2,1,0:T(8,128)S(1)} %get-tuple-element.68.wide, f32[2,24,128]{2,1,0:T(8,128)S(1)} %get-tuple-element.69.wide_pack, f32[2,8,24,128]{3,2,1,0:T(8,128)S(1)} %get-tuple-element.76.wide_broken, ...), custom_call_target="tpu_custom_call" | custom-call | tf_op jit(solution)/shard_map/weights_late/pallas_call | solution.py:721
  39.1 3.2 %force_late.3.inner = f32[3,8,16,128]{3,2,1,0:T(8,128)S(1)} custom-call(s32[6]{0:T(128)S(1)} %stack.36.edges, f32[3,8,16,128]{3,2,1,0:T(8,128)S(1)} %get-tuple-element.54.motion, f32[3,8,16,128]{3,2,1,0:T(8,128)S(1)} %get-tuple-element.74.early, f32[7,3,8,24,128]{4,3,2,1,0:T(8,128)S(1)} %get-tuple-element.75.early_shifts, ...), custom_call_target="tpu_custom_call" | custom-call | tf_op jit(solution)/shard_map/force_late/pallas_call | solution.py:721
  42.3 2.9 %collective-permute-done.8.x_high = f32[360,128]{1,0:T(8,128)S(1)} collective-permute-done((f32[360,128]{1,0:T(8,128)S(1)}, f32[360,128]{1,0:T(8,128)S(1)}, u32[]{:S(2)}, u32[]{:S(2)}) %collective-permute-start.8) | collective-permute-done | bytes 184352 | tf_op jit(solution)/shard_map/ppermute | solution.py:743
  45.2 1.9 %weights_outer.1 = (f32[280,8,128]{2,1,0:T(8,128)S(1)}, f32[3,8,16,128]{3,2,1,0:T(8,128)S(1)}) custom-call(s32[6]{0:T(128)S(1)} %stack.36.edges, f32[8,16,128]{2,1,0:T(8,128)S(1)} %get-tuple-element.55.stiffness, f32[8,16,128]{2,1,0:T(8,128)S(1)} %get-tuple-element.56.pore, f32[2,8,24,128]{3,2,1,0:T(8,128)S(1)} %get-tuple-element.68.wide, ...), custom_call_target="tpu_custom_call" | custom-call | tf_op jit(solution)/shard_map/weights_outer/pallas_call | solution.py:721
  47.1 2.2 %finish_first.1 = (f32[3,8,16,128]{3,2,1,0:T(8,128)S(1)}, f32[3,8,16,128]{3,2,1,0:T(8,128)S(1)}, f32[16,128]{1,0:T(8,128)S(1)}, f32[16,128]{1,0:T(8,128)S(1)}) custom-call(s32[6]{0:T(128)S(1)} %stack.36.edges, f32[3,8,16,128]{3,2,1,0:T(8,128)S(1)} %get-tuple-element.54.motion, f32[3,8,16,128]{3,2,1,0:T(8,128)S(1)} %copy-done, ...), custom_call_target="tpu_custom_call" | custom-call | tf_op jit(solution)/shard_map/finish_first/pallas_call | solution.py:721
  49.4 1.5 %collective-permute-start.10 = (f32[16,128]{1,0:T(8,128)S(1)}, f32[16,128]{1,0:T(8,128)S(1)}, u32[]{:S(2)}, u32[]{:S(2)}) collective-permute-start(f32[16,128]{1,0:T(8,128)S(1)} %get-tuple-element.82), channel_id=1, source_target_pairs={{0,3},{1,0},{2,1},{3,2},{4,7},{5,4},{6,5},{7,6},{8,11},{9,8},{10,9... | collective-permute-start | bytes 24584 | tf_op jit(solution)/shard_map/ppermute | solution.py:743
  50.9 1.0 %collective-permute-done.9.z_low = f32[16,128]{1,0:T(8,128)S(1)} collective-permute-done((f32[16,128]{1,0:T(8,128)S(1)}, f32[16,128]{1,0:T(8,128)S(1)}, u32[]{:S(2)}, u32[]{:S(2)}) %collective-permute-start.9) | collective-permute-done | bytes 8224 | tf_op jit(solution)/shard_map/ppermute | solution.py:743
  51.9 1.3 %collective-permute-done.10.z_high = f32[16,128]{1,0:T(8,128)S(1)} collective-permute-done((f32[16,128]{1,0:T(8,128)S(1)}, f32[16,128]{1,0:T(8,128)S(1)}, u32[]{:S(2)}, u32[]{:S(2)}) %collective-permute-start.10) | collective-permute-done | bytes 8224 | tf_op jit(solution)/shard_map/ppermute | solution.py:743
  53.9 3.6 %collective-permute-start.12 = (f32[80,128]{1,0:T(8,128)S(1)}, f32[80,128]{1,0:T(8,128)S(1)}, u32[]{:S(2)}, u32[]{:S(2)}) collective-permute-start(f32[80,128]{1,0:T(8,128)S(1)} %get-tuple-element.84), channel_id=1, source_target_pairs={{0,28},{4,0},{8,4},{12,8},{16,12},{20,16},{24,20},{28,24},{1,29},{... | collective-permute-start | bytes 122888 | tf_op jit(solution)/shard_map/ppermute | solution.py:743
  57.4 5.2 %force_early.4 = (f32[3,8,16,128]{3,2,1,0:T(8,128)S(1)}, f32[7,3,8,24,128]{4,3,2,1,0:T(8,128)S(1)}) custom-call(s32[6]{0:T(128)S(1)} %stack.36.edges, f32[3,8,16,128]{3,2,1,0:T(8,128)S(1)} %get-tuple-element.79.motion, f32[16,128]{1,0:T(8,128)S(1)} %collective-permute-done.9.z_low, f32[16,128]{1,0:T(8,128)S(1)} %collective-permute-done.10.z_high, ...), custom_call_target="tpu_custom_call" | custom-call | tf_op jit(solution)/shard_map/force_early/pallas_call | solution.py:721
  63.3 3.0 %collective-permute-start.13 = (f32[264,128]{1,0:T(8,128)S(1)}, f32[264,128]{1,0:T(8,128)S(1)}, u32[]{:S(2)}, u32[]{:S(2)}) collective-permute-start(f32[264,128]{1,0:T(8,128)S(1)} %get-tuple-element.90), channel_id=1, source_target_pairs={{0,32},{32,64},{64,96},{96,128},{128,160},{160,192},{192,224},{224... | collective-permute-start | bytes 405512 | tf_op jit(solution)/shard_map/ppermute | solution.py:743
  66.3 3.2 %force_late.4.inner = f32[3,8,16,128]{3,2,1,0:T(8,128)S(1)} custom-call(s32[6]{0:T(128)S(1)} %stack.36.edges, f32[3,8,16,128]{3,2,1,0:T(8,128)S(1)} %get-tuple-element.79.motion, f32[3,8,16,128]{3,2,1,0:T(8,128)S(1)} %get-tuple-element.86.early, f32[7,3,8,24,128]{4,3,2,1,0:T(8,128)S(1)} %get-tuple-element.87.early_shifts, ...), custom_call_target="tpu_custom_call" | custom-call | tf_op jit(solution)/shard_map/force_late/pallas_call | solution.py:721
  69.5 4.1 %collective-permute-done.14.x_high = f32[264,128]{1,0:T(8,128)S(1)} collective-permute-done((f32[264,128]{1,0:T(8,128)S(1)}, f32[264,128]{1,0:T(8,128)S(1)}, u32[]{:S(2)}, u32[]{:S(2)}) %collective-permute-start.14) | collective-permute-done | bytes 135200 | tf_op jit(solution)/shard_map/ppermute | solution.py:743
  73.6 2.2 %finish_middle.1 = (f32[3,8,16,128]{3,2,1,0:T(8,128)S(1)}, f32[3,8,16,128]{3,2,1,0:T(8,128)S(1)}, f32[16,128]{1,0:T(8,128)S(1)}, f32[16,128]{1,0:T(8,128)S(1)}) custom-call(s32[6]{0:T(128)S(1)} %stack.36.edges, f32[3,8,16,128]{3,2,1,0:T(8,128)S(1)} %get-tuple-element.79.motion, f32[3,8,16,128]{3,2,1,0:T(8,128)S(1)} %get-tuple-element.80.speed, ...), custom_call_target="tpu_custom_call" | custom-call | tf_op jit(solution)/shard_map/finish_middle/pallas_call | solution.py:721
  76.2 1.2 %collective-permute-start.16 = (f32[16,128]{1,0:T(8,128)S(1)}, f32[16,128]{1,0:T(8,128)S(1)}, u32[]{:S(2)}, u32[]{:S(2)}) collective-permute-start(f32[16,128]{1,0:T(8,128)S(1)} %get-tuple-element.95), channel_id=1, source_target_pairs={{0,3},{1,0},{2,1},{3,2},{4,7},{5,4},{6,5},{7,6},{8,11},{9,8},{10,9... | collective-permute-start | bytes 24584 | tf_op jit(solution)/shard_map/ppermute | solution.py:743
  77.4 1.0 %collective-permute-done.15.z_low = f32[16,128]{1,0:T(8,128)S(1)} collective-permute-done((f32[16,128]{1,0:T(8,128)S(1)}, f32[16,128]{1,0:T(8,128)S(1)}, u32[]{:S(2)}, u32[]{:S(2)}) %collective-permute-start.15) | collective-permute-done | bytes 8224 | tf_op jit(solution)/shard_map/ppermute | solution.py:743
  78.4 1.5 %collective-permute-done.16.z_high = f32[16,128]{1,0:T(8,128)S(1)} collective-permute-done((f32[16,128]{1,0:T(8,128)S(1)}, f32[16,128]{1,0:T(8,128)S(1)}, u32[]{:S(2)}, u32[]{:S(2)}) %collective-permute-start.16) | collective-permute-done | bytes 8224 | tf_op jit(solution)/shard_map/ppermute | solution.py:743
  80.8 3.6 %collective-permute-start.18 = (f32[80,128]{1,0:T(8,128)S(1)}, f32[80,128]{1,0:T(8,128)S(1)}, u32[]{:S(2)}, u32[]{:S(2)}) collective-permute-start(f32[80,128]{1,0:T(8,128)S(1)} %get-tuple-element.97), channel_id=1, source_target_pairs={{0,28},{4,0},{8,4},{12,8},{16,12},{20,16},{24,20},{28,24},{1,29},{... | collective-permute-start | bytes 122888 | tf_op jit(solution)/shard_map/ppermute | solution.py:743
  84.3 5.2 %force_early.5 = (f32[3,8,16,128]{3,2,1,0:T(8,128)S(1)}, f32[7,3,8,24,128]{4,3,2,1,0:T(8,128)S(1)}) custom-call(s32[6]{0:T(128)S(1)} %stack.36.edges, f32[3,8,16,128]{3,2,1,0:T(8,128)S(1)} %get-tuple-element.92.motion, f32[16,128]{1,0:T(8,128)S(1)} %collective-permute-done.15.z_low, f32[16,128]{1,0:T(8,128)S(1)} %collective-permute-done.16.z_high, ...), custom_call_target="tpu_custom_call" | custom-call | tf_op jit(solution)/shard_map/force_early/pallas_call | solution.py:721
  90.2 1.9 %collective-permute-start.19 = (f32[264,128]{1,0:T(8,128)S(1)}, f32[264,128]{1,0:T(8,128)S(1)}, u32[]{:S(2)}, u32[]{:S(2)}) collective-permute-start(f32[264,128]{1,0:T(8,128)S(1)} %get-tuple-element.103), channel_id=1, source_target_pairs={{0,32},{32,64},{64,96},{96,128},{128,160},{160,192},{192,224},{224... | collective-permute-start | bytes 405512 | tf_op jit(solution)/shard_map/ppermute | solution.py:743
  92.1 3.2 %force_late.5.inner = f32[3,8,16,128]{3,2,1,0:T(8,128)S(1)} custom-call(s32[6]{0:T(128)S(1)} %stack.36.edges, f32[3,8,16,128]{3,2,1,0:T(8,128)S(1)} %get-tuple-element.92.motion, f32[3,8,16,128]{3,2,1,0:T(8,128)S(1)} %get-tuple-element.99.early, f32[7,3,8,24,128]{4,3,2,1,0:T(8,128)S(1)} %get-tuple-element.100.early_shifts, ...), custom_call_target="tpu_custom_call" | custom-call | tf_op jit(solution)/shard_map/force_late/pallas_call | solution.py:721
  95.4 3.6 %collective-permute-done.20.x_high = f32[264,128]{1,0:T(8,128)S(1)} collective-permute-done((f32[264,128]{1,0:T(8,128)S(1)}, f32[264,128]{1,0:T(8,128)S(1)}, u32[]{:S(2)}, u32[]{:S(2)}) %collective-permute-start.20) | collective-permute-done | bytes 135200 | tf_op jit(solution)/shard_map/ppermute | solution.py:743
  99.0 2.9 %finish_last.1 = (f32[3,8,16,128]{3,2,1,0:T(8,128)}, f32[3,8,16,128]{3,2,1,0:T(8,128)}, f32[3,8,16,128]{3,2,1,0:T(8,128)}) custom-call(s32[6]{0:T(128)S(1)} %stack.36.edges, f32[3,8,16,128]{3,2,1,0:T(8,128)S(1)} %get-tuple-element.92.motion, f32[3,8,16,128]{3,2,1,0:T(8,128)S(1)} %get-tuple-element.93.speed, ...), custom_call_target="tpu_custom_call" | custom-call | tf_op jit(solution)/shard_map/finish_last/pallas_call | solution.py:721
  (33 shorter events, 5.9 us)
Async XLA Ops:
  4.5 27.9 %collective-permute-start.4 = (f32[1120,128]{1,0:T(8,128)S(1)}, f32[1120,128]{1,0:T(8,128)S(1)}, u32[]{:S(2)}, u32[]{:S(2)}) collective-permute-start(f32[1120,128]{1,0:T(8,128)S(1)} %get-tuple-element.61.x_up), channel_id=1, source_target_pairs={{0,32},{32,64},{64,96},{96,128},{128,160},{160,192},{192,224},{224... | collective-permute-start | bytes 1720328 | tf_op jit(solution)/shard_map/ppermute | solution.py:743
  9.3 23.1 %collective-permute-start.5 = (f32[368,128]{1,0:T(8,128)S(1)}, f32[368,128]{1,0:T(8,128)S(1)}, u32[]{:S(2)}, u32[]{:S(2)}) collective-permute-start(f32[368,128]{1,0:T(8,128)S(1)} %get-tuple-element.66), channel_id=1, source_target_pairs={{0,4},{4,8},{8,12},{12,16},{16,20},{20,24},{24,28},{28,0},{1,5},{5... | collective-permute-start | bytes 565256 | tf_op jit(solution)/shard_map/ppermute | solution.py:743
  10.1 4.4 %collective-permute-start = (f32[152,128]{1,0:T(8,128)S(1)}, f32[152,128]{1,0:T(8,128)S(1)}, u32[]{:S(2)}, u32[]{:S(2)}) collective-permute-start(f32[152,128]{1,0:T(8,128)S(1)} %get-tuple-element.57), channel_id=1, source_target_pairs={{0,1},{1,2},{2,3},{3,0},{4,5},{5,6},{6,7},{7,4},{8,9},{9,10},{10,1... | collective-permute-start | bytes 233480 | tf_op jit(solution)/shard_map/ppermute | solution.py:743
  10.3 4.6 %collective-permute-start.1 = (f32[152,128]{1,0:T(8,128)S(1)}, f32[152,128]{1,0:T(8,128)S(1)}, u32[]{:S(2)}, u32[]{:S(2)}) collective-permute-start(f32[152,128]{1,0:T(8,128)S(1)} %get-tuple-element.58), channel_id=1, source_target_pairs={{0,3},{1,0},{2,1},{3,2},{4,7},{5,4},{6,5},{7,6},{8,11},{9,8},{10,9... | collective-permute-start | bytes 233480 | tf_op jit(solution)/shard_map/ppermute | solution.py:743
  11.5 20.9 %collective-permute-start.6 = (f32[224,128]{1,0:T(8,128)S(1)}, f32[224,128]{1,0:T(8,128)S(1)}, u32[]{:S(2)}, u32[]{:S(2)}) collective-permute-start(f32[224,128]{1,0:T(8,128)S(1)} %get-tuple-element.67), channel_id=1, source_target_pairs={{0,28},{4,0},{8,4},{12,8},{16,12},{20,16},{24,20},{28,24},{1,29},{... | collective-permute-start | bytes 344072 | tf_op jit(solution)/shard_map/ppermute | solution.py:743
  15.5 16.9 %collective-permute-start.2 = (f32[176,128]{1,0:T(8,128)S(1)}, f32[176,128]{1,0:T(8,128)S(1)}, u32[]{:S(2)}, u32[]{:S(2)}) collective-permute-start(f32[176,128]{1,0:T(8,128)S(1)} %get-tuple-element.59), channel_id=1, source_target_pairs={{0,4},{4,8},{8,12},{12,16},{16,20},{20,24},{24,28},{28,0},{1,5},{5... | collective-permute-start | bytes 270344 | tf_op jit(solution)/shard_map/ppermute | solution.py:743
  17.3 15.1 %collective-permute-start.3 = (f32[176,128]{1,0:T(8,128)S(1)}, f32[176,128]{1,0:T(8,128)S(1)}, u32[]{:S(2)}, u32[]{:S(2)}) collective-permute-start(f32[176,128]{1,0:T(8,128)S(1)} %get-tuple-element.60), channel_id=1, source_target_pairs={{0,28},{4,0},{8,4},{12,8},{16,12},{20,16},{24,20},{28,24},{1,29},{... | collective-permute-start | bytes 270344 | tf_op jit(solution)/shard_map/ppermute | solution.py:743
  33.1 12.1 %collective-permute-start.7 = (f32[536,128]{1,0:T(8,128)S(1)}, f32[536,128]{1,0:T(8,128)S(1)}, u32[]{:S(2)}, u32[]{:S(2)}) collective-permute-start(f32[536,128]{1,0:T(8,128)S(1)} %get-tuple-element.71), channel_id=1, source_target_pairs={{0,32},{32,64},{64,96},{96,128},{128,160},{160,192},{192,224},{224... | collective-permute-start | bytes 823304 | tf_op jit(solution)/shard_map/ppermute | solution.py:743
  36.2 9.0 %collective-permute-start.8 = (f32[360,128]{1,0:T(8,128)S(1)}, f32[360,128]{1,0:T(8,128)S(1)}, u32[]{:S(2)}, u32[]{:S(2)}) collective-permute-start(f32[360,128]{1,0:T(8,128)S(1)} %get-tuple-element.72), channel_id=1, source_target_pairs={{0,224},{32,0},{64,32},{96,64},{128,96},{160,128},{192,160},{224,1... | collective-permute-start | bytes 552968 | tf_op jit(solution)/shard_map/ppermute | solution.py:743
  39.1 8.0 %copy-start = (f32[3,8,16,128]{3,2,1,0:T(8,128)S(1)}, f32[3,8,16,128]{3,2,1,0:T(8,128)}, u32[]{:S(2)}) copy-start(f32[3,8,16,128]{3,2,1,0:T(8,128)} %speed.1) | copy-start | bytes 589828
  49.3 2.6 %collective-permute-start.9 = (f32[16,128]{1,0:T(8,128)S(1)}, f32[16,128]{1,0:T(8,128)S(1)}, u32[]{:S(2)}, u32[]{:S(2)}) collective-permute-start(f32[16,128]{1,0:T(8,128)S(1)} %get-tuple-element.81), channel_id=1, source_target_pairs={{0,1},{1,2},{2,3},{3,0},{4,5},{5,6},{6,7},{7,4},{8,9},{9,10},{10,1... | collective-permute-start | bytes 24584 | tf_op jit(solution)/shard_map/ppermute | solution.py:743
  49.4 3.8 %collective-permute-start.10 = (f32[16,128]{1,0:T(8,128)S(1)}, f32[16,128]{1,0:T(8,128)S(1)}, u32[]{:S(2)}, u32[]{:S(2)}) collective-permute-start(f32[16,128]{1,0:T(8,128)S(1)} %get-tuple-element.82), channel_id=1, source_target_pairs={{0,3},{1,0},{2,1},{3,2},{4,7},{5,4},{6,5},{7,6},{8,11},{9,8},{10,9... | collective-permute-start | bytes 24584 | tf_op jit(solution)/shard_map/ppermute | solution.py:743
  53.8 8.9 %collective-permute-start.11 = (f32[80,128]{1,0:T(8,128)S(1)}, f32[80,128]{1,0:T(8,128)S(1)}, u32[]{:S(2)}, u32[]{:S(2)}) collective-permute-start(f32[80,128]{1,0:T(8,128)S(1)} %get-tuple-element.83), channel_id=1, source_target_pairs={{0,4},{4,8},{8,12},{12,16},{16,20},{20,24},{24,28},{28,0},{1,5},{5... | collective-permute-start | bytes 122888 | tf_op jit(solution)/shard_map/ppermute | solution.py:743
  53.9 8.8 %collective-permute-start.12 = (f32[80,128]{1,0:T(8,128)S(1)}, f32[80,128]{1,0:T(8,128)S(1)}, u32[]{:S(2)}, u32[]{:S(2)}) collective-permute-start(f32[80,128]{1,0:T(8,128)S(1)} %get-tuple-element.84), channel_id=1, source_target_pairs={{0,28},{4,0},{8,4},{12,8},{16,12},{20,16},{24,20},{28,24},{1,29},{... | collective-permute-start | bytes 122888 | tf_op jit(solution)/shard_map/ppermute | solution.py:743
  63.3 6.2 %collective-permute-start.13 = (f32[264,128]{1,0:T(8,128)S(1)}, f32[264,128]{1,0:T(8,128)S(1)}, u32[]{:S(2)}, u32[]{:S(2)}) collective-permute-start(f32[264,128]{1,0:T(8,128)S(1)} %get-tuple-element.90), channel_id=1, source_target_pairs={{0,32},{32,64},{64,96},{96,128},{128,160},{160,192},{192,224},{224... | collective-permute-start | bytes 405512 | tf_op jit(solution)/shard_map/ppermute | solution.py:743
  66.3 7.4 %collective-permute-start.14 = (f32[264,128]{1,0:T(8,128)S(1)}, f32[264,128]{1,0:T(8,128)S(1)}, u32[]{:S(2)}, u32[]{:S(2)}) collective-permute-start(f32[264,128]{1,0:T(8,128)S(1)} %get-tuple-element.91), channel_id=1, source_target_pairs={{0,224},{32,0},{64,32},{96,64},{128,96},{160,128},{192,160},{224,1... | collective-permute-start | bytes 405512 | tf_op jit(solution)/shard_map/ppermute | solution.py:743
  75.8 2.6 %collective-permute-start.15 = (f32[16,128]{1,0:T(8,128)S(1)}, f32[16,128]{1,0:T(8,128)S(1)}, u32[]{:S(2)}, u32[]{:S(2)}) collective-permute-start(f32[16,128]{1,0:T(8,128)S(1)} %get-tuple-element.94), channel_id=1, source_target_pairs={{0,1},{1,2},{2,3},{3,0},{4,5},{5,6},{6,7},{7,4},{8,9},{9,10},{10,1... | collective-permute-start | bytes 24584 | tf_op jit(solution)/shard_map/ppermute | solution.py:743
  76.2 3.7 %collective-permute-start.16 = (f32[16,128]{1,0:T(8,128)S(1)}, f32[16,128]{1,0:T(8,128)S(1)}, u32[]{:S(2)}, u32[]{:S(2)}) collective-permute-start(f32[16,128]{1,0:T(8,128)S(1)} %get-tuple-element.95), channel_id=1, source_target_pairs={{0,3},{1,0},{2,1},{3,2},{4,7},{5,4},{6,5},{7,6},{8,11},{9,8},{10,9... | collective-permute-start | bytes 24584 | tf_op jit(solution)/shard_map/ppermute | solution.py:743
  80.5 9.1 %collective-permute-start.17 = (f32[80,128]{1,0:T(8,128)S(1)}, f32[80,128]{1,0:T(8,128)S(1)}, u32[]{:S(2)}, u32[]{:S(2)}) collective-permute-start(f32[80,128]{1,0:T(8,128)S(1)} %get-tuple-element.96), channel_id=1, source_target_pairs={{0,4},{4,8},{8,12},{12,16},{16,20},{20,24},{24,28},{28,0},{1,5},{5... | collective-permute-start | bytes 122888 | tf_op jit(solution)/shard_map/ppermute | solution.py:743
  80.8 8.8 %collective-permute-start.18 = (f32[80,128]{1,0:T(8,128)S(1)}, f32[80,128]{1,0:T(8,128)S(1)}, u32[]{:S(2)}, u32[]{:S(2)}) collective-permute-start(f32[80,128]{1,0:T(8,128)S(1)} %get-tuple-element.97), channel_id=1, source_target_pairs={{0,28},{4,0},{8,4},{12,8},{16,12},{20,16},{24,20},{28,24},{1,29},{... | collective-permute-start | bytes 122888 | tf_op jit(solution)/shard_map/ppermute | solution.py:743
  90.2 5.2 %collective-permute-start.19 = (f32[264,128]{1,0:T(8,128)S(1)}, f32[264,128]{1,0:T(8,128)S(1)}, u32[]{:S(2)}, u32[]{:S(2)}) collective-permute-start(f32[264,128]{1,0:T(8,128)S(1)} %get-tuple-element.103), channel_id=1, source_target_pairs={{0,32},{32,64},{64,96},{96,128},{128,160},{160,192},{192,224},{224... | collective-permute-start | bytes 405512 | tf_op jit(solution)/shard_map/ppermute | solution.py:743
  92.1 6.9 %collective-permute-start.20 = (f32[264,128]{1,0:T(8,128)S(1)}, f32[264,128]{1,0:T(8,128)S(1)}, u32[]{:S(2)}, u32[]{:S(2)}) collective-permute-start(f32[264,128]{1,0:T(8,128)S(1)} %get-tuple-element.104), channel_id=1, source_target_pairs={{0,224},{32,0},{64,32},{96,64},{128,96},{160,128},{192,160},{224,1... | collective-permute-start | bytes 405512 | tf_op jit(solution)/shard_map/ppermute | solution.py:743
